TPU v7x, 128 devices: a whole 4x4x4 slice. The times are simulated.
128 devices in a mesh: seq: 4 (over x), ctx: 16 (over z, y), dp: 2 (over core).
Axes of the slice: x: 4, y: 4, z: 4, core: 2. Of those that a mesh axis runs over, the one named last changes fastest.
Arguments:
- tokens: bfloat16 [2, 8192, 768], P('dp', ('seq', 'ctx')), may hold values from -6 to 6
- qkv_weight: bfloat16 [768, 2304], P(('seq', 'ctx', 'dp')), may hold values from -0.3125 to 0.3125
- out_weight: bfloat16 [768, 768], P(('seq', 'ctx', 'dp')), may hold values from -0.875 to 0.875
- router_weight: bfloat16 [768, 32], P(('seq', 'ctx', 'dp')), may hold values from -0.15625 to 0.15625
- attn_gain: bfloat16 [768], P(('seq', 'ctx', 'dp')), may hold values from 0.5 to 1.5
- ffn_gain: bfloat16 [768], P(('seq', 'ctx', 'dp')), may hold values from 0.5 to 1.5
- query_bias: bfloat16 [768], P(('seq', 'ctx', 'dp')), may hold values from -3 to 3
- value_bias: bfloat16 [768], P(('seq', 'ctx', 'dp')), may hold values from -0.8984375 to 0.8984375
- out_bias: bfloat16 [768], P(('seq', 'ctx', 'dp')), may hold values from -1.1953125 to 1.1953125
- expert_in: bfloat16 [32, 768, 3072], P(('ctx', 'dp'), None, 'seq'), may hold values from -0.21875 to 0.21875
- expert_out: bfloat16 [32, 768, 3072], P(('ctx', 'dp'), None, 'seq'), may hold values from -0.109375 to 0.109375
- expert_ids: int32 [2, 8192, 2], P('dp', ('seq', 'ctx')), may hold values from 0 to 31, all different within a row; in each aligned block of 128 rows (0 to 127, 128 to 255, ..., all dimensions but the last counted through in order) at most 9 rows name the same one
- cotangent: bfloat16 [2, 8192, 768], P('dp', ('seq', 'ctx')), may hold values from -6 to 6
Outputs:
- mixed: bfloat16 [2, 8192, 768], P('dp', ('seq', 'ctx'))
- input_grad: bfloat16 [2, 8192, 768], P('dp', ('seq', 'ctx'))
- qkv_grad: float32 [768, 2304], P(('seq', 'ctx', 'dp'))
- out_grad: float32 [768, 768], P(('seq', 'ctx', 'dp'))
- router_grad: float32 [768, 32], P(('seq', 'ctx', 'dp'))
- attn_gain_grad: float32 [768], P(('seq', 'ctx', 'dp'))
- ffn_gain_grad: float32 [768], P(('seq', 'ctx', 'dp'))
- query_bias_grad: float32 [768], P(('seq', 'ctx', 'dp'))
- value_bias_grad: float32 [768], P(('seq', 'ctx', 'dp'))
- out_bias_grad: float32 [768], P(('seq', 'ctx', 'dp'))
- expert_in_grad: float32 [32, 768, 3072], P(('ctx', 'dp'), None, 'seq')
- expert_out_grad: float32 [32, 768, 3072], P(('ctx', 'dp'), None, 'seq')
Inputs may be any that keep to these rules, and one draw needn't show every extreme that they name: `expert_ids`: in the 128 rows of one device, no expert is named by more than 9 of the 2 choices of its tokens, and in every draw some expert is named exactly 9 times there; a token's 2 experts differ.
All inputs are finite; a program needn't handle non-finite values.
Results may differ from a plain program's by a relative error of at most 0.024.
Values may be sent and summed in bfloat16 or wider, within the bound.
No kernel may reach another device: no remote copies, remote signals or barrier semaphores. Data moves between devices by JAX's collectives and lax.ppermute only.
A program may use at most 128 MiB of HBM per device.

v0:
```python
import jax
import jax.numpy as jnp
from jax import lax
from jax.sharding import PartitionSpec as P

H = 12
HD = 64
TOPK = 2


EPS = 1e-06
MASKED = -1e30


def to_heads(values):
    return lax.all_to_all(values, "seq", split_axis=2, concat_axis=0, tiled=True)


def from_heads(values):
    return lax.all_to_all(values, "seq", split_axis=0, concat_axis=2, tiled=True)


def to_experts(values):
    return lax.all_to_all(values, ("ctx", "dp"), split_axis=0, concat_axis=0, tiled=True)


def from_experts(values):
    return lax.all_to_all(values, ("ctx", "dp"), split_axis=0, concat_axis=0, tiled=True)


def contract_rows(former, latter):
    return lax.dot_general(
        former, latter, (((0,), (0,)), ((), ())), preferred_element_type=jnp.float32
    )


def contract_cols(former, latter):
    return lax.dot_general(
        former, latter, (((1,), (1,)), ((), ())), preferred_element_type=jnp.float32
    )


def gelu_approx(values):
    return jax.nn.gelu(values, approximate=True)


def normed_parts(values, gains):
    factor = lax.rsqrt(jnp.mean(values * values, axis=-1, keepdims=True) + EPS)
    unit_rows = values * factor
    return (unit_rows * gains, unit_rows, factor)


def norm_back(grad_out, unit_rows, factor, gains):
    grad_unit = grad_out * gains
    grad_gain = jnp.sum(grad_out * unit_rows, axis=0)
    grad_in = factor * (
        grad_unit - unit_rows * jnp.mean(grad_unit * unit_rows, axis=-1, keepdims=True)
    )
    return (grad_in, grad_gain)


def scores_of(queries, key_rows, query_position, key_position):
    raw_scores = jnp.einsum(
        "qhd,khd->hqk", queries, key_rows, preferred_element_type=jnp.float32
    ) * HD ** (-0.5)
    return jnp.where(
        key_position[None, None, :] <= query_position[None, :, None], raw_scores, MASKED
    )


def per_device(
    tokens,
    qkv_weight,
    out_weight,
    router_weight,
    attn_gain,
    ffn_gain,
    query_bias,
    value_bias,
    out_bias,
    expert_in,
    expert_out,
    expert_ids,
    cotangent,
):
    qkv_full, out_full, router_full, gain_one, gain_two, bias_query, bias_value, bias_out = (
        lax.all_gather(qkv_weight, ("seq", "ctx", "dp"), axis=0, tiled=True),
        lax.all_gather(out_weight, ("seq", "ctx", "dp"), axis=0, tiled=True),
        lax.all_gather(router_weight, ("seq", "ctx", "dp"), axis=0, tiled=True),
        lax.all_gather(attn_gain, ("seq", "ctx", "dp"), axis=0, tiled=True),
        lax.all_gather(ffn_gain, ("seq", "ctx", "dp"), axis=0, tiled=True),
        lax.all_gather(query_bias, ("seq", "ctx", "dp"), axis=0, tiled=True),
        lax.all_gather(value_bias, ("seq", "ctx", "dp"), axis=0, tiled=True),
        lax.all_gather(out_bias, ("seq", "ctx", "dp"), axis=0, tiled=True),
    )
    width = tokens.shape[2]
    local_tokens = tokens.shape[1]
    groups = lax.axis_size("seq")
    places = lax.axis_size("ctx")
    heads_here = H // groups
    block_rows = groups * local_tokens
    gain_first = gain_one.astype(jnp.float32)
    gain_second = gain_two.astype(jnp.float32)
    residual = tokens.reshape(local_tokens, width).astype(jnp.float32)
    normed_one, unit_one, factor_one = normed_parts(residual, gain_first)
    first_in = normed_one.astype(jnp.bfloat16)
    projected = jnp.dot(first_in, qkv_full, preferred_element_type=jnp.float32)
    bias_row = jnp.concatenate(
        [
            bias_query.astype(jnp.float32),
            jnp.zeros((width,), jnp.float32),
            bias_value.astype(jnp.float32),
        ]
    )
    projected = (projected + bias_row[None, :]).astype(jnp.bfloat16).reshape(local_tokens, 3, width)
    headed = to_heads(projected)
    queries = headed[:, 0].reshape(block_rows, heads_here, HD)
    keyval_local = headed[:, 1:].reshape(block_rows, 2, heads_here, HD)
    keyval_all = lax.all_gather(keyval_local, "ctx", axis=0, tiled=True)
    ctx_place = lax.axis_index("ctx")
    row_index = jnp.arange(block_rows, dtype=jnp.int32)
    query_position = (
        row_index // local_tokens * places + ctx_place
    ) * local_tokens + row_index % local_tokens
    key_index = jnp.arange(places * block_rows, dtype=jnp.int32)
    key_position = (
        key_index % block_rows // local_tokens * places + key_index // block_rows
    ) * local_tokens + key_index % local_tokens
    key_blocks = keyval_all.reshape(places, block_rows, 2, heads_here, HD)
    position_blocks = key_position.reshape(places, block_rows)

    def track_peak(running, element):
        highest, totals = running
        block_keyval, block_position = element
        scores = scores_of(queries, block_keyval[:, 0], query_position, block_position)
        higher = jnp.maximum(highest, jnp.max(scores, axis=-1))
        totals = totals * jnp.exp(highest - higher) + jnp.sum(
            jnp.exp(scores - higher[..., None]), axis=-1
        )
        return ((higher, totals), None)

    start_peak = jnp.full((heads_here, block_rows), MASKED, jnp.float32)
    (highest, totals), unused = lax.scan(
        track_peak,
        (start_peak, jnp.zeros((heads_here, block_rows), jnp.float32)),
        (key_blocks, position_blocks),
    )
    log_total = highest + jnp.log(totals)

    def weigh_values(running, element):
        block_keyval, block_position = element
        scores = scores_of(queries, block_keyval[:, 0], query_position, block_position)
        probs = jnp.exp(scores - log_total[..., None]).astype(jnp.bfloat16)
        return (
            running
            + jnp.einsum(
                "hqk,khd->qhd", probs, block_keyval[:, 1], preferred_element_type=jnp.float32
            ),
            None,
        )

    attended, unused = lax.scan(
        weigh_values,
        jnp.zeros((block_rows, heads_here, HD), jnp.float32),
        (key_blocks, position_blocks),
    )
    attended = attended.astype(jnp.bfloat16).reshape(block_rows, 1, width // groups)
    mixed_heads = from_heads(attended).reshape(local_tokens, width)
    branch_out = (
        jnp.dot(mixed_heads, out_full, preferred_element_type=jnp.float32)
        + bias_out.astype(jnp.float32)[None, :]
    )
    middle = residual + branch_out
    normed_two, unit_two, factor_two = normed_parts(middle, gain_second)
    second_in = normed_two.astype(jnp.bfloat16)
    logits = jnp.dot(second_in, router_full, preferred_element_type=jnp.float32)
    experts = router_full.shape[1]
    capacity = max(2, local_tokens * TOPK * 9 // (8 * experts))
    routes = expert_ids.reshape(local_tokens, TOPK)
    flat_routes = routes.reshape(-1)
    expert_cols = jnp.arange(experts, dtype=jnp.int32)
    onehot = (flat_routes[:, None] == expert_cols[None, :]).astype(jnp.int32)
    slots = jnp.sum((jnp.cumsum(onehot, axis=0) - 1) * onehot, axis=1)
    target = flat_routes * capacity + slots
    chosen = jnp.take_along_axis(logits, routes, axis=1)
    weights_raw = jnp.exp(chosen - jnp.max(chosen, axis=1, keepdims=True))
    gates = weights_raw / jnp.sum(weights_raw, axis=1, keepdims=True)
    outgoing = (
        jnp.zeros((experts * capacity, width), jnp.bfloat16)
        .at[target]
        .set(jnp.repeat(second_in, TOPK, axis=0))
    )
    received = to_experts(outgoing.reshape(experts, capacity, width)).reshape(
        experts * capacity, width
    )
    inner_full, outer_full = (
        lax.all_gather(expert_in[0], "seq", axis=1, tiled=True),
        lax.all_gather(expert_out[0], "seq", axis=1, tiled=True),
    )
    pre_act = jnp.dot(received, inner_full, preferred_element_type=jnp.float32)
    activated = gelu_approx(pre_act).astype(jnp.bfloat16)
    produced = contract_cols(activated, outer_full).astype(jnp.bfloat16)
    returned = from_experts(produced.reshape(experts, capacity, width)).reshape(
        experts * capacity, width
    )
    picked = returned[target].reshape(local_tokens, TOPK, width).astype(jnp.float32)
    result = middle + jnp.sum(gates[..., None] * picked, axis=1)
    gradient = cotangent.reshape(local_tokens, width).astype(jnp.float32)
    picked_grad = (gates[..., None] * gradient[:, None, :]).astype(jnp.bfloat16)
    gate_grad = jnp.sum(gradient[:, None, :] * picked, axis=-1)
    chosen_grad = gates * (gate_grad - jnp.sum(gates * gate_grad, axis=1, keepdims=True))
    logit_grad = jnp.sum(
        jnp.where(routes[:, :, None] == expert_cols[None, None, :], chosen_grad[:, :, None], 0.0),
        axis=1,
    ).astype(jnp.bfloat16)
    router_grad = contract_rows(second_in, logit_grad)
    second_grad = contract_cols(logit_grad, router_full)
    back_out = (
        jnp.zeros((experts * capacity, width), jnp.bfloat16)
        .at[target]
        .set(picked_grad.reshape(-1, width))
    )
    arrived = to_experts(back_out.reshape(experts, capacity, width)).reshape(
        experts * capacity, width
    )
    act_grad = jnp.dot(arrived, outer_full, preferred_element_type=jnp.float32)
    unused, gelu_pull = jax.vjp(gelu_approx, pre_act)
    pre_grad = gelu_pull(act_grad)[0].astype(jnp.bfloat16)
    input_rows = contract_cols(pre_grad, inner_full).astype(jnp.bfloat16)
    inner_grad, outer_grad = (
        lax.psum_scatter(
            contract_rows(received, pre_grad).astype(jnp.bfloat16),
            "seq",
            scatter_dimension=1,
            tiled=True,
        ).astype(jnp.float32),
        lax.psum_scatter(
            contract_rows(arrived, activated).astype(jnp.bfloat16),
            "seq",
            scatter_dimension=1,
            tiled=True,
        ).astype(jnp.float32),
    )
    sent_back = from_experts(input_rows.reshape(experts, capacity, width)).reshape(
        experts * capacity, width
    )
    second_grad = second_grad + jnp.sum(
        sent_back[target].reshape(local_tokens, TOPK, width).astype(jnp.float32), axis=1
    )
    middle_part, gain_two_grad = norm_back(second_grad, unit_two, factor_two, gain_second)
    middle_grad = gradient + middle_part
    branch_grad = middle_grad.astype(jnp.bfloat16)
    out_bias_grad = jnp.sum(branch_grad.astype(jnp.float32), axis=0)
    out_grad = contract_rows(mixed_heads, branch_grad)
    heads_grad = (
        contract_cols(branch_grad, out_full).astype(jnp.bfloat16).reshape(local_tokens, 1, width)
    )
    attended_grad = to_heads(heads_grad).reshape(block_rows, heads_here, HD)

    def probs_and_grads(block_keyval, block_position):
        scores = scores_of(queries, block_keyval[:, 0], query_position, block_position)
        probs = jnp.exp(scores - log_total[..., None])
        prob_grad = jnp.einsum(
            "qhd,khd->hqk", attended_grad, block_keyval[:, 1], preferred_element_type=jnp.float32
        )
        return (probs, prob_grad)

    def measure(running, element):
        probs, prob_grad = probs_and_grads(element[0], element[1])
        return (running + jnp.sum(probs * prob_grad, axis=-1), None)

    deltas, unused = lax.scan(
        measure, jnp.zeros((heads_here, block_rows), jnp.float32), (key_blocks, position_blocks)
    )

    def score_grads(block_keyval, block_position):
        probs, prob_grad = probs_and_grads(block_keyval, block_position)
        return (probs, (probs * (prob_grad - deltas[..., None])).astype(jnp.bfloat16))

    def pull_queries(running, element):
        probs, score_grad = score_grads(element[0], element[1])
        return (
            running
            + jnp.einsum(
                "hqk,khd->qhd", score_grad, element[0][:, 0], preferred_element_type=jnp.float32
            )
            * HD ** (-0.5),
            None,
        )

    query_grad, unused = lax.scan(
        pull_queries,
        jnp.zeros((block_rows, heads_here, HD), jnp.float32),
        (key_blocks, position_blocks),
    )
    block_keyval = keyval_all.reshape(
        block_rows * lax.axis_size("ctx") // block_rows, block_rows, 2, heads_here, HD
    )
    block_position = key_position.reshape(
        block_rows * lax.axis_size("ctx") // block_rows, block_rows
    )

    def one_block(element):
        probs, score_grad = score_grads(element[0], element[1])
        key_grad = jnp.einsum(
            "hqk,qhd->khd", score_grad, queries, preferred_element_type=jnp.float32
        ) * HD ** (-0.5)
        value_grad = jnp.einsum(
            "hqk,qhd->khd",
            probs.astype(jnp.bfloat16),
            attended_grad,
            preferred_element_type=jnp.float32,
        )
        return jnp.stack([key_grad, value_grad], axis=1)

    keyval_grad = lax.psum_scatter(
        lax.map(one_block, (block_keyval, block_position))
        .reshape(block_rows * lax.axis_size("ctx"), 2, heads_here, HD)
        .astype(jnp.bfloat16),
        "ctx",
        scatter_dimension=0,
        tiled=True,
    )
    grads_heads = jnp.concatenate(
        [
            query_grad.astype(jnp.bfloat16).reshape(block_rows, 1, width // groups),
            keyval_grad.reshape(block_rows, 2, width // groups),
        ],
        axis=1,
    )
    projected_grad = from_heads(grads_heads).reshape(local_tokens, 3 * width)
    query_bias_grad = jnp.sum(projected_grad[:, :width].astype(jnp.float32), axis=0)
    value_bias_grad = jnp.sum(projected_grad[:, 2 * width :].astype(jnp.float32), axis=0)
    qkv_grad = contract_rows(first_in, projected_grad)
    first_grad = contract_cols(projected_grad, qkv_full)
    input_part, gain_one_grad = norm_back(first_grad, unit_one, factor_one, gain_first)
    input_grad = middle_grad + input_part
    shares = (
        lax.psum_scatter(qkv_grad, ("seq", "ctx", "dp"), scatter_dimension=0, tiled=True),
        lax.psum_scatter(out_grad, ("seq", "ctx", "dp"), scatter_dimension=0, tiled=True),
        lax.psum_scatter(router_grad, ("seq", "ctx", "dp"), scatter_dimension=0, tiled=True),
        lax.psum_scatter(gain_one_grad, ("seq", "ctx", "dp"), scatter_dimension=0, tiled=True),
        lax.psum_scatter(gain_two_grad, ("seq", "ctx", "dp"), scatter_dimension=0, tiled=True),
        lax.psum_scatter(query_bias_grad, ("seq", "ctx", "dp"), scatter_dimension=0, tiled=True),
        lax.psum_scatter(value_bias_grad, ("seq", "ctx", "dp"), scatter_dimension=0, tiled=True),
        lax.psum_scatter(out_bias_grad, ("seq", "ctx", "dp"), scatter_dimension=0, tiled=True),
    )
    return (
        result.astype(jnp.bfloat16).reshape(tokens.shape),
        input_grad.astype(jnp.bfloat16).reshape(tokens.shape),
        shares[0],
        shares[1],
        shares[2],
        shares[3],
        shares[4],
        shares[5],
        shares[6],
        shares[7],
        inner_grad[None],
        outer_grad[None],
    )


def solution(mesh):
    return jax.shard_map(
        per_device,
        mesh=mesh,
        in_specs=(
            P("dp", ("seq", "ctx"), None),
            P(("seq", "ctx", "dp"), None),
            P(("seq", "ctx", "dp"), None),
            P(("seq", "ctx", "dp"), None),
            P(("seq", "ctx", "dp")),
            P(("seq", "ctx", "dp")),
            P(("seq", "ctx", "dp")),
            P(("seq", "ctx", "dp")),
            P(("seq", "ctx", "dp")),
            P(("ctx", "dp"), None, "seq"),
            P(("ctx", "dp"), None, "seq"),
            P("dp", ("seq", "ctx"), None),
            P("dp", ("seq", "ctx"), None),
        ),
        out_specs=(
            P("dp", ("seq", "ctx"), None),
            P("dp", ("seq", "ctx"), None),
            P(("seq", "ctx", "dp"), None),
            P(("seq", "ctx", "dp"), None),
            P(("seq", "ctx", "dp"), None),
            P(("seq", "ctx", "dp")),
            P(("seq", "ctx", "dp")),
            P(("seq", "ctx", "dp")),
            P(("seq", "ctx", "dp")),
            P(("seq", "ctx", "dp")),
            P(("ctx", "dp"), None, "seq"),
            P(("ctx", "dp"), None, "seq"),
        ),
        check_vma=False,
    )
```

profile of v0, /device:TPU:0, one launch (start us, length us, event | category | flops | bytes accessed | tf_op | source)
XLA Modules:
  0.0 1601.1 jit_solution(7591776688530087638)
XLA Ops:
  12.2 69.4 %all-reduce.16 = (bf16[768]{0:T(1024)(128)(2,1)S(1)}, bf16[768]{0:T(1024)(128)(2,1)S(1)}, bf16[768]{0:T(1024)(128)(2,1)S(1)}, bf16[768]{0:T(1024)(128)(2,1)}, bf16[768]{0:T(1024)(128)(2,1)}) all-reduce(bf16[768]{0:T(1024)(128)(2,1)S(1)} %dynamic-update-slice.2, ...), channel_id=1, replica_groups=mesh['seq'=4,'ctx'=16,'dp'=2] {'seq','ctx','dp'}, use_global_device_ids=true, to_apply=%add.2 | all-reduce | flops 3840 | bytes 15360
  83.2 5.0 reshape.639
  94.7 14.7 all_to_all.83
  117.5 33.5 %all-gather.4 = bf16[128,6,32]{2,1,0:T(8,128)(2,1)S(1)} all-gather(bf16[1,6,32]{2,1,0:T(8,128)(2,1)S(1)} %bitcast.452), channel_id=1, replica_groups=mesh['seq'=4,'ctx'=16,'dp'=2] {'seq','ctx','dp'}, dimensions={0}, use_global_device_ids=true | all-gather | bytes 49536 | tf_op jit(solution)/shard_map/all_gather | solution.py:89
  152.7 22.5 %all-gather.11.cloned.1.call-done = bf16[8192,2,3,64]{0,3,2,1:T(8,128)(2,1)} async-done(((bf16[512,2,3,64]{0,3,2,1:T(8,128)(2,1)}), bf16[8192,2,3,64]{0,3,2,1:T(8,128)(2,1)}) %all-gather.11.cloned.1.call-update) | async-done | bytes 6291472 | tf_op jit(solution)/shard_map/all_gather | solution.py:119
  175.2 6.4 copy.179
  181.5 73.7 %while.58 = (s32[]{:T(128)}, f32[3,512]{1,0:T(4,128)S(1)}, f32[3,512]{1,0:T(4,128)S(1)}, s32[16,512]{1,0:T(8,128)}, bf16[16,512,2,3,64]{1,4,3,2,0:T(8,128)(2,1)}...) while((s32[]{:T(128)}, f32[3,512]{1,0:T(4,128)S(1)}, ...), condition=%wide.region_4.5_spmd.clone, body=%wide.region_1.4_spmd.clone.sunk | while | flops 106446336 | bytes 9396376 | solution.py:143
  255.9 80.5 %while.59 = (s32[]{:T(128)}, f32[512,3,64]{0,2,1:T(8,128)}, bf16[16,512,2,3,64]{1,4,3,2,0:T(8,128)(2,1)}, s32[16,512]{1,0:T(8,128)}, bf16[512,3,64]{0,2,1:T(8,12...) while((s32[]{:T(128)}, f32[512,3,64]{0,2,1:T(8,128)}, ...), condition=%wide.region_6.7_spmd.clone, body=%wide.region_5.6_spmd.clone.sunk | while | flops 204939264 | bytes 2703483 | solution.py:162
  356.4 6.3 all-to-all-start.2
  371.0 6.3 all-to-all-done.2
  382.9 13.6 all-to-all-done.4
  397.8 6.0 fusion.117
  403.8 6.9 fusion.126
  418.9 6.4 fusion.132
  427.4 6.0 all-to-all-done.5
  433.5 4.6 all-to-all-start.3
  443.6 9.1 all-to-all-done.3
  471.8 6.1 all-to-all-done.6
  479.0 76.1 %while.60 = (s32[]{:T(128)}, f32[3,512]{1,0:T(4,128)S(1)}, s32[16,512]{1,0:T(8,128)}, bf16[16,512,2,3,64]{1,4,3,2,0:T(8,128)(2,1)}, bf16[512,3,64]{0,2,1:T(8,128...) while((s32[]{:T(128)}, f32[3,512]{1,0:T(4,128)S(1)}, ...), condition=%wide.region_23.24_spmd.clone, body=%wide.region_21.23_spmd.clone.sunk | while | flops 205530624 | bytes 8429699 | solution.py:272
  555.1 189.5 %while.57 = (s32[]{:T(128)}, bf16[16,512,2,3,64]{1,4,3,2,0:T(8,128)(2,1)}, s32[16,512]{1,0:T(8,128)}, bf16[16,512,2,3,64]{1,4,3,2,0:T(8,128)(2,1)}, bf16[512,3,6...) while((s32[]{:T(128)}, ...), condition=%wide.region_27.28_spmd.clone, body=%wide.region_26.27_spmd.clone.sunk | while | flops 411770880 | bytes 16021685 | solution.py:317
  744.7 6.4 copy.175
  758.6 6.9 convolution_convert_fusion
  765.5 122.8 %while.61 = (s32[]{:T(128)}, f32[512,3,64]{0,2,1:T(8,128)}, bf16[16,512,2,3,64]{1,4,3,2,0:T(8,128)(2,1)}, s32[16,512]{1,0:T(8,128)}, bf16[512,3,64]{0,2,1:T(8,12...) while((s32[]{:T(128)}, f32[512,3,64]{0,2,1:T(8,128)}, ...), condition=%wide.region_25.26_spmd.clone, body=%wide.region_24.25_spmd.clone.sunk | while | flops 307273728 | bytes 10967207 | solution.py:291
  897.6 13.1 all-to-all-done.7
  916.3 385.1 %fusion.196 = (f32[8,2304]{1,0:T(8,128)}, f32[8,768]{1,0:T(8,128)}) fusion(f32[768,2304]{1,0:T(8,128)} %fusion.160, f32[768,768]{1,0:T(8,128)S(1)} %fusion.192), kind=kCustom, calls=%all-reduce-scatter.2 | all-reduce-scatter fusion | flops 3145729 | bytes 9535488
  1319.2 12.9 collective-permute-start.54
  1340.7 4.7 collective-permute-start.49
  1369.2 4.7 collective-permute-start.38
  1378.2 4.8 collective-permute-start.35
  1461.6 63.4 %all-reduce.15 = (f32[768]{0:T(1024)S(1)}, f32[768]{0:T(1024)S(1)}, f32[768]{0:T(1024)S(1)}, f32[768]{0:T(1024)S(1)}, f32[768]{0:T(1024)S(1)}) all-reduce(f32[768]{0:T(1024)} %get-tuple-element.595, f32[768]{0:T(1024)S(1)} %get-tuple-element.591, ...), channel_id=8, replica_groups=mesh['seq'=4,'ctx'=16,'dp'=2] {'seq','ctx','dp'}, use_global_device_ids=true, to_apply=%region_34.35.clone | all-reduce | flops 3840 | bytes 30720
  1528.0 27.9 %concatenate.12 = f32[262,768]{1,0:T(8,128)S(1)} concatenate(f32[6,768]{1,0:T(8,128)} %copy-done.40, f32[8,768]{1,0:T(8,128)} %collective-permute-done.62, f32[8,768]{1,0:T(8,128)} %collective-permute-done.61, f32[8,768]{1,0:T(8,128)} %collective-permute-done.60, f32[8,768]{1,0:T(8,128)} %collective-permute-done.59, f32[8,768]{1,0:T(8,128)} %collective-permute-done.58, ...), dimensions={0} | concatenate | bytes 1609728
  1573.2 20.3 %concatenate.11 = f32[262,2304]{1,0:T(8,128)S(1)} concatenate(f32[6,2304]{1,0:T(8,128)} %collective-permute-done.31, f32[8,2304]{1,0:T(8,128)} %collective-permute-done.30, f32[8,2304]{1,0:T(8,128)} %collective-permute-done.29, f32[8,2304]{1,0:T(8,128)} %collective-permute-done.28, f32[8,2304]{1,0:T(8,128)} %collective-permute-done.27, f32[8,2304]{1,0:T(8,128)} %collective-permute-done.26, ...), dimensions={0} | concatenate | bytes 4829184
  (1088 shorter events, 808.8 us)
Async XLA Ops:
  7.2 76.1 %all-gather.17.cloned.1.call-start = ((), (), s32[]{:S(2)}) async-start(), calls=%async_computation.17 | async-start | bytes 4755456 | tf_op jit(solution)/shard_map/all_gather | solution.py:87
  7.9 167.3 %all-gather.11.cloned.1.call-start = ((), (), s32[]{:S(2)}) async-start(), calls=%async_computation.11 | async-start | bytes 6684672 | tf_op jit(solution)/shard_map/all_gather | solution.py:119
  110.4 234.0 %all-gather.19.cloned.1.call-start = ((), (), s32[]{:S(2)}) async-start(), calls=%async_computation.18 | async-start | bytes 1585152 | tf_op jit(solution)/shard_map/all_gather | solution.py:88
  111.1 286.7 %all-gather.13.cloned.1.call-start = ((), (), s32[]{:S(2)}) async-start(), calls=%async_computation.15 | async-start | bytes 5898240 | tf_op jit(solution)/shard_map/all_gather | solution.py:197
  111.7 292.1 %all-gather.15.cloned.1.call-start = ((), (), s32[]{:S(2)}) async-start(), calls=%async_computation.16 | async-start | bytes 5898240 | tf_op jit(solution)/shard_map/all_gather | solution.py:198
  356.4 20.9 %all-to-all-start.2 = ((bf16[32,9,768]{2,1,0:T(8,128)(2,1)}), bf16[32,9,768]{2,1,0:T(8,128)(2,1)S(1)}, u32[]{:S(2)}, u32[]{:S(2)}) async-start(bf16[32,9,768]{2,1,0:T(8,128)(2,1)} %reshape.566), calls=%async_computation.2 | async-start | bytes 1572864 | tf_op jit(solution)/shard_map/all_to_all | solution.py:24
  377.3 19.2 %all-to-all-start.4 = ((bf16[32,9,768]{2,1,0:T(8,128)(2,1)}), bf16[32,9,768]{2,1,0:T(8,128)(2,1)}, u32[]{:S(2)}, u32[]{:S(2)}) async-start(bf16[32,9,768]{2,1,0:T(8,128)(2,1)} %reshape.571), calls=%async_computation.4 | async-start | bytes 1572864 | tf_op jit(solution)/shard_map/all_to_all | solution.py:24
  414.6 18.9 %all-to-all-start.5 = ((bf16[32,9,768]{2,1,0:T(8,128)(2,1)}), bf16[32,9,768]{2,1,0:T(8,128)(2,1)S(1)}, u32[]{:S(2)}, u32[]{:S(2)}) async-start(bf16[32,9,768]{2,1,0:T(8,128)(2,1)} %reshape.573), calls=%async_computation.5 | async-start | bytes 1572864 | tf_op jit(solution)/shard_map/all_to_all | solution.py:28
  433.5 19.2 %all-to-all-start.3 = ((bf16[32,9,768]{2,1,0:T(8,128)(2,1)}), bf16[32,9,768]{2,1,0:T(8,128)(2,1)}, u32[]{:S(2)}, u32[]{:S(2)}) async-start(bf16[32,9,768]{2,1,0:T(8,128)(2,1)} %reshape.568), calls=%async_computation.3 | async-start | bytes 1572864 | tf_op jit(solution)/shard_map/all_to_all | solution.py:28
  471.6 417.8 %reduce-scatter.8.cloned.1.call-start = ((), (), s32[]{:S(2)}) async-start(), calls=%async_computation.12 | async-start | bytes 6684672 | tf_op jit(solution)/shard_map/reduce_scatter | solution.py:316
  751.1 631.9 %all-reduce.20.cloned.1.call-start = ((), (), s32[]{:S(2)}) async-start(), calls=%async_computation.19 | async-start | bytes 786432
  753.0 643.8 %reduce-scatter.10.cloned.1.call-start = ((), (), s32[]{:S(2)}) async-start(), calls=%async_computation.13 | async-start | bytes 5898240 | tf_op jit(solution)/shard_map/reduce_scatter | solution.py:231
  757.6 651.7 %reduce-scatter.12.cloned.1.call-start = ((), (), s32[]{:S(2)}) async-start(), calls=%async_computation.14 | async-start | bytes 5898240 | tf_op jit(solution)/shard_map/reduce_scatter | solution.py:237
  891.8 18.9 %all-to-all-start.7 = ((bf16[512,3,192]{2,1,0:T(4,128)(2,1)}), bf16[512,3,192]{2,1,0:T(4,128)(2,1)}, u32[]{:S(2)}, u32[]{:S(2)}) async-start(bf16[512,3,192]{2,1,0:T(4,128)(2,1)} %copy.162), calls=%async_computation.8 | async-start | bytes 2097152 | tf_op jit(solution)/shard_map/all_to_all | solution.py:20
  1311.6 20.5 %collective-permute-start.58 = (f32[8,768]{1,0:T(8,128)}, f32[8,768]{1,0:T(8,128)}, u32[]{:S(2)}, u32[]{:S(2)}) collective-permute-start(f32[8,768]{1,0:T(8,128)} %get-tuple-element.692), channel_id=1, source_target_pairs={{0,27},{1,28},{2,29},{3,30},{4,31},{5,32},{6,33},{7,34},{8,35},{9,... | collective-permute-start | bytes 73736
  1313.5 21.1 %collective-permute-start.57 = (f32[8,768]{1,0:T(8,128)}, f32[8,768]{1,0:T(8,128)}, u32[]{:S(2)}, u32[]{:S(2)}) collective-permute-start(f32[8,768]{1,0:T(8,128)} %get-tuple-element.692), channel_id=1, source_target_pairs={{0,26},{1,27},{2,28},{3,29},{4,30},{5,31},{6,32},{7,33},{8,34},{9,... | collective-permute-start | bytes 73736
  1315.4 21.1 %collective-permute-start.56 = (f32[8,768]{1,0:T(8,128)}, f32[8,768]{1,0:T(8,128)}, u32[]{:S(2)}, u32[]{:S(2)}) collective-permute-start(f32[8,768]{1,0:T(8,128)} %get-tuple-element.692), channel_id=1, source_target_pairs={{0,25},{1,26},{2,27},{3,28},{4,29},{5,30},{6,31},{7,32},{8,33},{9,... | collective-permute-start | bytes 73736
  1317.3 21.5 %collective-permute-start.55 = (f32[8,768]{1,0:T(8,128)}, f32[8,768]{1,0:T(8,128)}, u32[]{:S(2)}, u32[]{:S(2)}) collective-permute-start(f32[8,768]{1,0:T(8,128)} %get-tuple-element.692), channel_id=1, source_target_pairs={{0,24},{1,25},{2,26},{3,27},{4,28},{5,29},{6,30},{7,31},{8,32},{9,... | collective-permute-start | bytes 73736
  1319.2 21.5 %collective-permute-start.54 = (f32[8,768]{1,0:T(8,128)}, f32[8,768]{1,0:T(8,128)}, u32[]{:S(2)}, u32[]{:S(2)}) collective-permute-start(f32[8,768]{1,0:T(8,128)} %get-tuple-element.692), channel_id=1, source_target_pairs={{0,23},{1,24},{2,25},{3,26},{4,27},{5,28},{6,29},{7,30},{8,31},{9,... | collective-permute-start | bytes 73736
  1362.9 15.3 collective-permute-start.40
  1365.8 20.2 %collective-permute-start.39 = (f32[8,768]{1,0:T(8,128)}, f32[8,768]{1,0:T(8,128)}, u32[]{:S(2)}, u32[]{:S(2)}) collective-permute-start(f32[8,768]{1,0:T(8,128)} %get-tuple-element.692), channel_id=1, source_target_pairs={{0,8},{1,9},{2,10},{3,11},{4,12},{5,13},{6,14},{7,15},{8,16},{9,17... | collective-permute-start | bytes 73736
  1369.2 19.0 %collective-permute-start.38 = (f32[8,768]{1,0:T(8,128)}, f32[8,768]{1,0:T(8,128)}, u32[]{:S(2)}, u32[]{:S(2)}) collective-permute-start(f32[8,768]{1,0:T(8,128)} %get-tuple-element.692), channel_id=1, source_target_pairs={{0,7},{1,8},{2,9},{3,10},{4,11},{5,12},{6,13},{7,14},{8,15},{9,16}... | collective-permute-start | bytes 73736
  1373.8 16.2 %collective-permute-start.37 = (f32[8,768]{1,0:T(8,128)}, f32[8,768]{1,0:T(8,128)}, u32[]{:S(2)}, u32[]{:S(2)}) collective-permute-start(f32[8,768]{1,0:T(8,128)} %get-tuple-element.692), channel_id=1, source_target_pairs={{0,6},{1,7},{2,8},{3,9},{4,10},{5,11},{6,12},{7,13},{8,14},{9,15},... | collective-permute-start | bytes 73736
  1375.7 16.2 %collective-permute-start.36 = (f32[8,768]{1,0:T(8,128)}, f32[8,768]{1,0:T(8,128)}, u32[]{:S(2)}, u32[]{:S(2)}) collective-permute-start(f32[8,768]{1,0:T(8,128)} %get-tuple-element.692), channel_id=1, source_target_pairs={{0,5},{1,6},{2,7},{3,8},{4,9},{5,10},{6,11},{7,12},{8,13},{9,14},{... | collective-permute-start | bytes 73736
  1378.2 16.7 %collective-permute-start.35 = (f32[8,768]{1,0:T(8,128)}, f32[8,768]{1,0:T(8,128)}, u32[]{:S(2)}, u32[]{:S(2)}) collective-permute-start(f32[8,768]{1,0:T(8,128)} %get-tuple-element.692), channel_id=1, source_target_pairs={{0,4},{1,5},{2,6},{3,7},{4,8},{5,9},{6,10},{7,11},{8,12},{9,13},{1... | collective-permute-start | bytes 73736
  1385.9 21.4 %collective-permute-start.30 = (f32[8,2304]{1,0:T(8,128)}, f32[8,2304]{1,0:T(8,128)}, u32[]{:S(2)}, u32[]{:S(2)}) collective-permute-start(f32[8,2304]{1,0:T(8,128)} %get-tuple-element.691), channel_id=1, source_target_pairs={{0,31},{1,32},{2,33},{3,34},{4,35},{5,36},{6,37},{7,38},{8,39},{9,... | collective-permute-start | bytes 221192
  1447.8 108.2 %collective-permute-start.9 = (f32[8,2304]{1,0:T(8,128)}, f32[8,2304]{1,0:T(8,128)S(1)}, u32[]{:S(2)}, u32[]{:S(2)}) collective-permute-start(f32[8,2304]{1,0:T(8,128)} %get-tuple-element.691), channel_id=1, source_target_pairs={{0,10},{1,11},{2,12},{3,13},{4,14},{5,15},{6,16},{7,17},{8,18},{9,... | collective-permute-start | bytes 221192
  1449.9 108.7 %collective-permute-start.8 = (f32[8,2304]{1,0:T(8,128)}, f32[8,2304]{1,0:T(8,128)S(1)}, u32[]{:S(2)}, u32[]{:S(2)}) collective-permute-start(f32[8,2304]{1,0:T(8,128)} %get-tuple-element.691), channel_id=1, source_target_pairs={{0,9},{1,10},{2,11},{3,12},{4,13},{5,14},{6,15},{7,16},{8,17},{9,1... | collective-permute-start | bytes 221192
  1453.5 109.7 %collective-permute-start.7 = (f32[8,2304]{1,0:T(8,128)}, f32[8,2304]{1,0:T(8,128)S(1)}, u32[]{:S(2)}, u32[]{:S(2)}) collective-permute-start(f32[8,2304]{1,0:T(8,128)} %get-tuple-element.691), channel_id=1, source_target_pairs={{0,8},{1,9},{2,10},{3,11},{4,12},{5,13},{6,14},{7,15},{8,16},{9,17... | collective-permute-start | bytes 221192
  1455.6 108.9 %collective-permute-start.6 = (f32[8,2304]{1,0:T(8,128)}, f32[8,2304]{1,0:T(8,128)S(1)}, u32[]{:S(2)}, u32[]{:S(2)}) collective-permute-start(f32[8,2304]{1,0:T(8,128)} %get-tuple-element.691), channel_id=1, source_target_pairs={{0,7},{1,8},{2,9},{3,10},{4,11},{5,12},{6,13},{7,14},{8,15},{9,16}... | collective-permute-start | bytes 221192
  1459.9 108.2 %collective-permute-start.5 = (f32[8,2304]{1,0:T(8,128)}, f32[8,2304]{1,0:T(8,128)S(1)}, u32[]{:S(2)}, u32[]{:S(2)}) collective-permute-start(f32[8,2304]{1,0:T(8,128)} %get-tuple-element.691), channel_id=1, source_target_pairs={{0,6},{1,7},{2,8},{3,9},{4,10},{5,11},{6,12},{7,13},{8,14},{9,15},... | collective-permute-start | bytes 221192
  1555.9 16.0 collective-permute-start.4
  (165 other events, 1417.3 us)
Sparse Core Ops, SparseCore 0:
  11.1 69.7 all-gather.16
  110.5 64.6 all-gather.10
  178.0 63.4 all-gather.18
  243.0 49.9 all-gather.12
  294.5 53.2 all-gather.14
  751.3 77.4 reduce-scatter.7
  834.0 143.6 all-reduce.19
  980.0 54.6 reduce-scatter.9
  1037.1 57.2 reduce-scatter.11
where the time goes:
time: 1630 us; the launch traced here: 1600 us
  blocking collectives  566 us (35%)
  matrix products  322 us (20%)
  local copies, waits for them, and re-layouts  303 us (19%)
  starting transfers between devices  195 us (12%)
  other arithmetic  113 us (7%)
  waiting for transfers between devices  83.3 us (5%)
    unnamed x3, blocking collectives  518 us
    unnamed x65, starting transfers between devices  162 us
    squeeze x80, local copies, waits for them, and re-layouts, per_device(): lax.scan(track_peak, (start_peak, jnp.zeros((heads_here, block_rows), jnp...  83.7 us
    unnamed x138, local copies, waits for them, and re-layouts  76.4 us
    dynamic_slice x80, local copies, waits for them, and re-layouts, per_device(): lax.scan(track_peak, (start_peak, jnp.zeros((heads_here, block_rows), jnp...  58.3 us
    dot_general x16, matrix products, pull_queries(): jnp.einsum('hqk,khd->qhd', score_grad, element[0][:, 0], preferred_elemen...  57.4 us
    dot_general x16, matrix products, one_block(): jnp.einsum('hqk,qhd->khd', score_grad, queries, preferred_element_type=jn...  54 us
    dot_general x16, matrix products, weigh_values(): jnp.einsum('hqk,khd->qhd', probs, block_keyval[:, 1], preferred_element_t...  48.6 us
  transfers between devices with their start and end apart: 80, of which 8 were waited for; matrix products, arithmetic and copies ran while one was open for 48% of the time, Pallas kernels for 0%

commit v1 on v0

v1 whole, which is shorter than its diff:
```python
import functools

import jax
import jax.numpy as jnp
import numpy as np
from jax import lax
from jax.experimental import pallas as pl
from jax.experimental.pallas import tpu as pltpu
from jax.sharding import PartitionSpec as P

H = 12
HD = 64
TOPK = 2
D = 768
T = 128
NS = 4
HL = H // NS
HW = HL * HD
QR = NS * T
CD = 32
CAP = 9
SLOTS = 24
ROWS = CD * SLOTS
LINES = CD * CAP
PACK = 208

EPS = 1e-06
MASKED = -1e30
BF = jnp.bfloat16
F32 = jnp.float32

VMEM = pl.BlockSpec(memory_space=pltpu.VMEM)
SMEM = pl.BlockSpec(memory_space=pltpu.SMEM)


def dot(former, latter, former_dim, latter_dim):
    return lax.dot_general(
        former,
        latter,
        (((former_dim,), (latter_dim,)), ((), ())),
        preferred_element_type=F32,
    )


def params(**more):
    return pltpu.CompilerParams(vmem_limit_bytes=56 * 1024 * 1024, **more)


def shift_seq(values, steps):
    return lax.ppermute(values, "seq", [(i, (i + steps) % NS) for i in range(NS)])


def shift_z(values, steps):
    pairs = [(z * NS + y, (z + steps) % NS * NS + y) for z in range(NS) for y in range(NS)]
    return lax.ppermute(values, "ctx", pairs)


def shift_y(values, steps):
    pairs = [(z * NS + y, z * NS + (y + steps) % NS) for z in range(NS) for y in range(NS)]
    return lax.ppermute(values, "ctx", pairs)


def collect(values, shift):
    return [values] + [shift(values, -i) for i in range(1, NS)]


def deliver(pieces, shift):
    return [pieces[0]] + [shift(pieces[i], i) for i in range(1, NS)]


def swap_seq(values):
    return lax.all_to_all(values, "seq", split_axis=0, concat_axis=0, tiled=True)


def swap_experts(values):
    return lax.all_to_all(values, ("ctx", "dp"), split_axis=0, concat_axis=0, tiled=True)


def gather_seq(values):
    place = lax.axis_index("seq")
    whole = jnp.zeros((NS,) + values.shape, values.dtype)
    for i, piece in enumerate(collect(values, shift_seq)):
        whole = lax.dynamic_update_slice(whole, piece[None], ((place + i) % NS, 0, 0))
    return whole


def scatter_seq(values):
    place = lax.axis_index("seq")
    pieces = [
        lax.dynamic_slice(values, ((place + i) % NS, 0, 0), (1,) + values.shape[1:])[0]
        for i in range(NS)
    ]
    return deliver(pieces, shift_seq)


def tile_of(refs, rows, j):
    return jnp.concatenate([ref[rows, j * T : (j + 1) * T] for ref in refs], axis=1)


def causal_tile(place_ref):
    z, y = place_ref[0], place_ref[1]
    k_index = lax.broadcasted_iota(jnp.int32, (QR, QR), 0)
    q_index = lax.broadcasted_iota(jnp.int32, (QR, QR), 1)
    k_place = z * QR + (((y + (k_index >> 7)) & 3) << 7) + (k_index & 127)
    q_place = (((z + (q_index >> 7)) & 3) << 9) + y * T + (q_index & 127)
    return k_place <= q_place


def split3(values):
    high = values.astype(BF).astype(F32)
    middle = (values - high).astype(BF).astype(F32)
    return high, middle, values - high - middle


def attend_kernel(place_ref, *refs):
    q_refs, kv_refs, o_refs = refs[0:4], refs[4:8], refs[8:12]
    lse_ref, bias_ref = refs[12], refs[13]
    bias_ref[...] = jnp.where(causal_tile(place_ref), 0.0, MASKED)

    def head(h, carry):
        rows = pl.ds(pl.multiple_of(h * HD, HD), HD)
        v_rows = pl.ds(pl.multiple_of(HW + h * HD, HD), HD)
        for j in range(NS):
            q_tile = tile_of(q_refs, rows, j)
            top = total = acc = None
            for jp in range(j + 1):
                k_tile = tile_of(kv_refs, rows, jp)
                v_tile = tile_of(kv_refs, v_rows, jp)
                scores = dot(k_tile, q_tile, 0, 0)
                if jp == j:
                    scores = jnp.where(bias_ref[...] < 0.0, MASKED, scores)
                here = jnp.max(scores, axis=0, keepdims=True)
                if jp == 0:
                    top = here
                    probs = jnp.exp(scores - top)
                    total = jnp.sum(probs, axis=0, keepdims=True)
                    acc = dot(v_tile, probs.astype(BF), 1, 0)
                else:
                    higher = jnp.maximum(top, here)
                    fade = jnp.exp(top - higher)
                    probs = jnp.exp(scores - higher)
                    total = total * fade + jnp.sum(probs, axis=0, keepdims=True)
                    acc = acc * fade + dot(v_tile, probs.astype(BF), 1, 0)
                    top = higher
            out = (acc / total).astype(BF)
            lse = top + jnp.log(total)
            for i in range(NS):
                o_refs[i][rows, j * T : (j + 1) * T] = out[:, i * T : (i + 1) * T]
                lse_ref[h, i : i + 1, j * T : (j + 1) * T] = lse[:, i * T : (i + 1) * T]
        return carry

    lax.fori_loop(0, HL, head, 0)
    for i in range(NS):
        logs = jnp.concatenate([lse_ref[h, i : i + 1, :] for h in range(HL)], axis=0)
        high, middle, low = split3(logs)
        rest = jnp.zeros((PACK - HW - 3 * HL, QR), F32)
        o_refs[i][HW:PACK, :] = jnp.concatenate([high, middle, low, rest], axis=0).astype(BF)


def attend(place, queries, keyvals):
    return pl.pallas_call(
        attend_kernel,
        out_shape=[jax.ShapeDtypeStruct((PACK, QR), BF)] * NS,
        in_specs=[SMEM] + [VMEM] * 8,
        out_specs=[VMEM] * NS,
        scratch_shapes=[pltpu.VMEM((HL, 8, QR), F32), pltpu.VMEM((QR, QR), F32)],
        compiler_params=params(),
        cost_estimate=pl.CostEstimate(
            flops=4 * 30 * QR * QR * HD, bytes_accessed=4 << 20, transcendentals=30 * QR * QR
        ),
        name="attend",
    )(place, *queries, *keyvals)


def lse_of(stats):
    return stats[0:HL] + stats[HL : 2 * HL] + stats[2 * HL : 3 * HL]


def merge_kernel(*refs):
    parts, o_ref, stat_ref = refs[0:4], refs[4], refs[5]
    logs = [lse_of(part[HW:PACK, :].astype(F32)) for part in parts]
    top = functools.reduce(jnp.maximum, logs)
    lse = top + jnp.log(functools.reduce(jnp.add, [jnp.exp(log - top) for log in logs]))
    shares = [jnp.exp(log - lse) for log in logs]
    for h in range(HL):
        rows = slice(h * HD, (h + 1) * HD)
        o_ref[rows, :] = functools.reduce(
            jnp.add,
            [part[rows, :].astype(F32) * share[h : h + 1] for part, share in zip(parts, shares)],
        ).astype(BF)
    stat_ref[...] = jnp.concatenate([lse, jnp.zeros((8 - HL, QR), F32)], axis=0)


def merge(parts):
    return pl.pallas_call(
        merge_kernel,
        out_shape=[jax.ShapeDtypeStruct((HW, QR), BF), jax.ShapeDtypeStruct((8, QR), F32)],
        in_specs=[VMEM] * 4,
        out_specs=[VMEM] * 2,
        compiler_params=params(),
        name="merge",
    )(*parts)


def grad_heads_kernel(db_ref, w_ref, o_ref, lse_ref, out_ref):
    grads = dot(w_ref[...], db_ref[...], 1, 1).astype(BF)
    out_ref[0:HW, :] = grads
    product = grads.astype(F32) * o_ref[...].astype(F32)
    delta = jnp.concatenate(
        [jnp.sum(product[h * HD : (h + 1) * HD], axis=0, keepdims=True) for h in range(HL)], axis=0
    )
    high, middle, low = split3(lse_ref[0:HL, :])
    d_high, d_middle, unused = split3(delta)
    rest = jnp.zeros((PACK - HW - 5 * HL, QR), F32)
    out_ref[HW:PACK, :] = jnp.concatenate(
        [high, middle, low, d_high, d_middle, rest], axis=0
    ).astype(BF)


def grad_heads(rows, weight, attended, lse):
    return pl.pallas_call(
        grad_heads_kernel,
        out_shape=jax.ShapeDtypeStruct((PACK, QR), BF),
        in_specs=[VMEM] * 4,
        out_specs=VMEM,
        compiler_params=params(),
        name="grad_heads",
    )(rows, weight, attended, lse)


def attend_back_kernel(place_ref, *refs):
    q_refs, kv_refs, do_refs = refs[0:4], refs[4:8], refs[8:12]
    dq_refs, dkv_refs = refs[12:16], refs[16:20]
    lse_ref, delta_ref, bias_ref, dq_ref = refs[20:24]
    bias_ref[...] = jnp.where(causal_tile(place_ref), 0.0, MASKED)
    for i in range(NS):
        stats = do_refs[i][HW:PACK, :].astype(F32)
        logs = lse_of(stats)
        deltas = stats[3 * HL : 4 * HL] + stats[4 * HL : 5 * HL]
        for h in range(HL):
            lse_ref[h, i : i + 1, :] = logs[h : h + 1]
            delta_ref[h, i : i + 1, :] = deltas[h : h + 1]

    def head(h, carry):
        rows = pl.ds(pl.multiple_of(h * HD, HD), HD)
        v_rows = pl.ds(pl.multiple_of(HW + h * HD, HD), HD)

        def stat(ref, j):
            return jnp.concatenate(
                [ref[h, i : i + 1, j * T : (j + 1) * T] for i in range(NS)], axis=1
            )

        for jp in range(NS):
            k_tile = tile_of(kv_refs, rows, jp)
            v_tile = tile_of(kv_refs, v_rows, jp)
            dk = dv = None
            for j in range(jp, NS):
                q_tile = tile_of(q_refs, rows, j)
                do_tile = tile_of(do_refs, rows, j)
                scores = dot(k_tile, q_tile, 0, 0)
                if jp == j:
                    scores = jnp.where(bias_ref[...] < 0.0, MASKED, scores)
                probs = jnp.exp(scores - stat(lse_ref, j))
                slopes = dot(v_tile, do_tile, 0, 0)
                ds = (probs * (slopes - stat(delta_ref, j))).astype(BF)
                dv_here = dot(do_tile, probs.astype(BF), 1, 1)
                dk_here = dot(q_tile, ds, 1, 1)
                dq_here = dot(k_tile, ds, 1, 0)
                dv = dv_here if dv is None else dv + dv_here
                dk = dk_here if dk is None else dk + dk_here
                if jp == 0:
                    dq_ref[j] = dq_here
                else:
                    dq_ref[j] += dq_here
            dk, dv = dk.astype(BF), dv.astype(BF)
            for i in range(NS):
                dkv_refs[i][rows, jp * T : (jp + 1) * T] = dk[:, i * T : (i + 1) * T]
                dkv_refs[i][v_rows, jp * T : (jp + 1) * T] = dv[:, i * T : (i + 1) * T]
        for j in range(NS):
            dq = (dq_ref[j] * HD ** (-0.5)).astype(BF)
            for i in range(NS):
                dq_refs[i][rows, j * T : (j + 1) * T] = dq[:, i * T : (i + 1) * T]
        return carry

    lax.fori_loop(0, HL, head, 0)


def attend_back(place, queries, keyvals, grads):
    out = pl.pallas_call(
        attend_back_kernel,
        out_shape=[jax.ShapeDtypeStruct((HW, QR), BF)] * NS
        + [jax.ShapeDtypeStruct((2 * HW, QR), BF)] * NS,
        in_specs=[SMEM] + [VMEM] * 12,
        out_specs=[VMEM] * 8,
        scratch_shapes=[
            pltpu.VMEM((HL, 8, QR), F32),
            pltpu.VMEM((HL, 8, QR), F32),
            pltpu.VMEM((QR, QR), F32),
            pltpu.VMEM((NS, HD, QR), F32),
        ],
        compiler_params=params(),
        cost_estimate=pl.CostEstimate(
            flops=10 * 30 * QR * QR * HD, bytes_accessed=6 << 20, transcendentals=30 * QR * QR
        ),
        name="attend_back",
    )(place, *queries, *keyvals, *grads)
    return out[0:NS], out[NS:]


def pick_rows(target, offset):
    lines = lax.broadcasted_iota(jnp.int32, (T, ROWS), 1)
    return (lines == target + offset).astype(F32).astype(BF)


def norm_two(middle):
    factor = lax.rsqrt(jnp.mean(middle * middle, axis=-1, keepdims=True) + EPS)
    return middle * factor, factor


def route_kernel(
    x_ref, branch_ref, small_ref, router_ref, ids_ref, cot_ref,
    out_ref, m_ref, a_ref, gate_ref, target_ref,
):
    branch = functools.reduce(jnp.add, [branch_ref[i].astype(F32) for i in range(NS)])
    middle = x_ref[...].astype(F32) + branch + small_ref[2:3, :]
    unit, factor = norm_two(middle)
    second = (unit * small_ref[1:2, :]).astype(BF)
    logits = dot(second, router_ref[...], 1, 0)
    cols = lax.broadcasted_iota(jnp.int32, (T, CD), 1)
    named = [(ids_ref[:, k : k + 1] == cols).astype(F32) for k in range(TOPK)]
    earlier = lax.broadcasted_iota(jnp.int32, (T, T), 1) < lax.broadcasted_iota(
        jnp.int32, (T, T), 0
    )
    counts = dot(earlier.astype(F32).astype(BF), (named[0] + named[1]).astype(BF), 1, 0)
    chosen = [jnp.sum(name * logits, axis=1, keepdims=True) for name in named]
    top = jnp.maximum(chosen[0], chosen[1])
    raw = [jnp.exp(value - top) for value in chosen]
    gates = [value / (raw[0] + raw[1]) for value in raw]
    slots = [jnp.sum(name * counts, axis=1, keepdims=True).astype(jnp.int32) for name in named]
    targets = [ids_ref[:, k : k + 1] * SLOTS + slots[k] for k in range(TOPK)]
    grads = cot_ref[...].astype(F32)
    places = jnp.concatenate(
        [pick_rows(targets[0], 0) + pick_rows(targets[1], 0)]
        + [pick_rows(targets[k], CAP) for k in range(TOPK)],
        axis=0,
    )
    values = jnp.concatenate([second] + [(gates[k] * grads).astype(BF) for k in range(TOPK)], axis=0)
    out_ref[...] = dot(places, values, 0, 0).astype(BF)
    m_ref[...] = middle
    a_ref[...] = second
    gate_ref[...] = jnp.concatenate(gates, axis=1)
    target_ref[...] = jnp.concatenate(targets, axis=1)


def route(rows, branch, small, router, ids, cotangent):
    return pl.pallas_call(
        route_kernel,
        out_shape=[
            jax.ShapeDtypeStruct((ROWS, D), BF),
            jax.ShapeDtypeStruct((T, D), F32),
            jax.ShapeDtypeStruct((T, D), BF),
            jax.ShapeDtypeStruct((T, TOPK), F32),
            jax.ShapeDtypeStruct((T, TOPK), jnp.int32),
        ],
        in_specs=[VMEM] * 6,
        out_specs=[VMEM] * 5,
        compiler_params=params(),
        name="route",
    )(rows, branch, small, router, ids, cotangent)


GELU_A = float(np.sqrt(2.0 / np.pi))
GELU_B = 0.044715


def expert_kernel(
    rows_ref, pick_ref, win_ref, wout_ref, out_ref, gin_ref, gout_ref, a_ref, dy_ref, y_ref, da_ref
):
    step = pl.program_id(0)

    @pl.when(step == 0)
    def first():
        both = dot(pick_ref[...], rows_ref[...], 1, 0).astype(BF)
        a_ref[...] = both[0:LINES]
        dy_ref[...] = both[LINES:]

    rows, grads = a_ref[...], dy_ref[...]
    inner, outer = win_ref[0], wout_ref[0]
    pre = dot(rows, inner, 1, 0)
    square = pre * pre
    bent = jnp.tanh(GELU_A * pre * (1.0 + GELU_B * square))
    act = (0.5 * pre * (1.0 + bent)).astype(BF)
    slope = 0.5 * (1.0 + bent) + 0.5 * pre * (1.0 - bent * bent) * (
        GELU_A * (1.0 + 3.0 * GELU_B * square)
    )
    pre_grad = (dot(grads, outer, 1, 0) * slope).astype(BF)
    made = dot(act, outer, 1, 1)
    back = dot(pre_grad, inner, 1, 1)
    gin_ref[0] = dot(rows, pre_grad, 0, 0).astype(BF)
    gout_ref[0] = dot(grads, act, 0, 0).astype(BF)

    @pl.when(step == 0)
    def start():
        y_ref[...] = made
        da_ref[...] = back

    @pl.when(step > 0)
    def more():
        y_ref[...] += made
        da_ref[...] += back

    @pl.when(step == pl.num_programs(0) - 1)
    def last():
        both = jnp.concatenate([y_ref[...].astype(BF), da_ref[...].astype(BF)], axis=0)
        out_ref[...] = dot(pick_ref[...], both, 0, 0).astype(BF)


def expert_pick():
    lines = np.arange(LINES)
    pick = np.zeros((2 * LINES, ROWS), np.float32)
    pick[lines, lines // CAP * SLOTS + lines % CAP] = 1.0
    pick[LINES + lines, lines // CAP * SLOTS + CAP + lines % CAP] = 1.0
    return pick


def expert(rows, inner, outer):
    tile = 384
    halves = D // tile

    def weight_spec():
        return pl.BlockSpec((1, D, tile), lambda i: (i // halves, 0, i % halves))

    def whole(*shape):
        return pl.BlockSpec(shape, lambda i: (0, 0))

    return pl.pallas_call(
        expert_kernel,
        grid=(NS * halves,),
        out_shape=[
            jax.ShapeDtypeStruct((ROWS, D), BF),
            jax.ShapeDtypeStruct((NS, D, D), BF),
            jax.ShapeDtypeStruct((NS, D, D), BF),
        ],
        in_specs=[whole(ROWS, D), whole(2 * LINES, ROWS), weight_spec(), weight_spec()],
        out_specs=[whole(ROWS, D), weight_spec(), weight_spec()],
        scratch_shapes=[
            pltpu.VMEM((LINES, D), BF),
            pltpu.VMEM((LINES, D), BF),
            pltpu.VMEM((LINES, D), F32),
            pltpu.VMEM((LINES, D), F32),
        ],
        compiler_params=params(dimension_semantics=("arbitrary",)),
        cost_estimate=pl.CostEstimate(
            flops=12 * LINES * D * 4 * D, bytes_accessed=20 << 20, transcendentals=LINES * 4 * D
        ),
        name="expert",
    )(rows, jnp.asarray(expert_pick(), BF), inner, outer)


def settle_kernel(
    back_ref, m_ref, a_ref, gate_ref, target_ref, ids_ref, cot_ref, small_ref, router_ref,
    mixed_ref, db_ref, dm_ref, rg_ref, sums_ref,
):
    back = back_ref[...]
    targets = [target_ref[:, k : k + 1] for k in range(TOPK)]
    picked = [dot(pick_rows(target, 0), back, 1, 0) for target in targets]
    returned = dot(pick_rows(targets[0], CAP) + pick_rows(targets[1], CAP), back, 1, 0)
    middle = m_ref[...]
    grads = cot_ref[...].astype(F32)
    gates = [gate_ref[:, k : k + 1] for k in range(TOPK)]
    mixed_ref[...] = (middle + gates[0] * picked[0] + gates[1] * picked[1]).astype(BF)
    gate_grads = [jnp.sum(grads * value, axis=1, keepdims=True) for value in picked]
    mean = gates[0] * gate_grads[0] + gates[1] * gate_grads[1]
    cols = lax.broadcasted_iota(jnp.int32, (T, CD), 1)
    logit_grad = functools.reduce(
        jnp.add,
        [
            jnp.where(ids_ref[:, k : k + 1] == cols, gates[k] * (gate_grads[k] - mean), 0.0)
            for k in range(TOPK)
        ],
    ).astype(BF)
    rg_ref[...] = dot(a_ref[...], logit_grad, 0, 0)
    second_grad = dot(logit_grad, router_ref[...], 1, 1) + returned
    unit, factor = norm_two(middle)
    weighted = second_grad * small_ref[1:2, :]
    whole = grads + factor * (weighted - unit * jnp.mean(weighted * unit, axis=-1, keepdims=True))
    dm_ref[...] = whole
    rounded = whole.astype(BF)
    db_ref[...] = rounded
    sums_ref[...] = jnp.concatenate(
        [
            jnp.sum(second_grad * unit, axis=0, keepdims=True),
            jnp.sum(rounded.astype(F32), axis=0, keepdims=True),
            jnp.zeros((6, D), F32),
        ],
        axis=0,
    )


def settle(back, middle, second, gates, targets, ids, cotangent, small, router):
    return pl.pallas_call(
        settle_kernel,
        out_shape=[
            jax.ShapeDtypeStruct((T, D), BF),
            jax.ShapeDtypeStruct((T, D), BF),
            jax.ShapeDtypeStruct((T, D), F32),
            jax.ShapeDtypeStruct((D, CD), F32),
            jax.ShapeDtypeStruct((8, D), F32),
        ],
        in_specs=[VMEM] * 9,
        out_specs=[VMEM] * 5,
        compiler_params=params(),
        name="settle",
    )(back, middle, second, gates, targets, ids, cotangent, small, router)


def order_constant():
    order = np.zeros((D, D), np.float32)
    for g in range(D):
        s, rest = divmod(g, HW)
        c, i = divmod(rest, 6)
        order[g, c * 24 + s * 6 + i] = 1.0
    return order


def spread(rows, width):
    return jnp.pad(rows, [(0, 0)] * (rows.ndim - 1) + [(0, width - rows.shape[-1])])


def per_device(
    tokens,
    qkv_weight,
    out_weight,
    router_weight,
    attn_gain,
    ffn_gain,
    query_bias,
    value_bias,
    out_bias,
    expert_in,
    expert_out,
    expert_ids,
    cotangent,
):
    order = jnp.asarray(order_constant(), BF)
    ctx = lax.axis_index("ctx")
    place = jnp.stack([ctx // NS, ctx % NS]).astype(jnp.int32)
    rows = tokens.reshape(T, D)
    ids = expert_ids.reshape(T, TOPK)
    cot = cotangent.reshape(T, D)

    inner = lax.all_gather(expert_in[0], "seq", axis=0, tiled=False)
    outer = lax.all_gather(expert_out[0], "seq", axis=0, tiled=False)

    columns = qkv_weight.reshape(6, 3, NS, HW).transpose(2, 0, 1, 3).reshape(NS, 6, 3 * HW)
    extras = jnp.concatenate(
        [router_weight, attn_gain[:, None], ffn_gain[:, None], out_bias[:, None]], axis=1
    )
    sent = spread(
        jnp.concatenate([columns, jnp.broadcast_to(extras[None], (NS, 6, CD + 3))], axis=2), D
    )
    arrived = swap_seq(sent).reshape(NS * 6, D)
    mine = jnp.concatenate(
        [arrived, out_weight, spread(query_bias[None], D), spread(value_bias[None], D)], axis=0
    )
    everything = swap_experts(jnp.broadcast_to(mine[None], (CD, 32, D)))
    weights = everything[:, :24].reshape(D, D)
    sorted_weights = dot(order, weights, 1, 0).astype(BF)
    qkv = sorted_weights[:, : 3 * HW]
    router = sorted_weights[:, 3 * HW : 3 * HW + CD]
    small = dot(weights[:, 3 * HW + CD : 3 * HW + CD + 8], order, 0, 1)
    out_mine = everything[:, 24:30].reshape(HW, D)
    bias = jnp.concatenate(
        [
            everything[:, 30, :6].reshape(HW),
            jnp.zeros((HW,), BF),
            everything[:, 31, :6].reshape(HW),
        ]
    ).astype(F32)

    stream = gather_seq(rows).reshape(QR, D).astype(F32)
    factor = lax.rsqrt(jnp.mean(stream * stream, axis=-1, keepdims=True) + EPS)
    unit = stream * factor
    first_in = (unit * small[0:1]).astype(BF)
    projected = (dot(qkv, first_in, 0, 1) + bias[:, None]).astype(BF)
    queries = collect(projected[:HW] * jnp.asarray(HD ** (-0.5), BF), shift_z)
    keyvals = collect(projected[HW:], shift_y)
    attended, lse = merge(deliver(attend(place, queries, keyvals), shift_z))
    branch = swap_seq(dot(attended, out_mine, 0, 0).astype(BF).reshape(NS, T, D))

    outgoing, middle, second, gates, targets = route(rows, branch, small, router, ids, cot)
    received = swap_experts(outgoing.reshape(CD, SLOTS, D)).reshape(ROWS, D)
    made, inner_grad, outer_grad = expert(received, inner, outer)
    returned = swap_experts(made.reshape(CD, SLOTS, D)).reshape(ROWS, D)
    inner_grad = lax.psum_scatter(inner_grad, "seq", scatter_dimension=0, tiled=False)
    outer_grad = lax.psum_scatter(outer_grad, "seq", scatter_dimension=0, tiled=False)
    mixed, branch_grad, middle_grad, router_grad, sums = settle(
        returned, middle, second, gates, targets, ids, cot, small, router
    )

    branch_grads = gather_seq(branch_grad).reshape(QR, D)
    out_grad = dot(attended, branch_grads, 1, 0)
    heads_grad = collect(grad_heads(branch_grads, out_mine, attended, lse), shift_z)
    query_parts, keyval_parts = attend_back(place, queries, keyvals, heads_grad)
    query_grad = sum(part.astype(F32) for part in deliver(query_parts, shift_z))
    keyval_grad = sum(part.astype(F32) for part in deliver(keyval_parts, shift_y))
    projected_grad = jnp.concatenate([query_grad, keyval_grad], axis=0).astype(BF)

    first_grad = dot(projected_grad, qkv, 0, 1)
    gain_grad = jnp.sum(first_grad * unit, axis=0, keepdims=True)
    parts = scatter_seq(first_grad.astype(BF).reshape(NS, T, D))
    mine_grad = sum(part.astype(F32) for part in parts)
    own = rows.astype(F32)
    own_factor = lax.rsqrt(jnp.mean(own * own, axis=-1, keepdims=True) + EPS)
    own_unit = own * own_factor
    weighted = mine_grad * small[0:1]
    input_grad = middle_grad + own_factor * (
        weighted - own_unit * jnp.mean(weighted * own_unit, axis=-1, keepdims=True)
    )

    arrived_in = dot(first_in, order, 1, 0).astype(BF)
    qkv_grad = dot(arrived_in, projected_grad, 0, 1).astype(BF)
    lines = jnp.concatenate([gain_grad, sums[0:2]], axis=0).astype(BF)
    extra_grads = jnp.concatenate(
        [dot(order, router_grad.astype(BF), 0, 0), dot(order, lines, 0, 1)], axis=1
    ).astype(BF)
    main = spread(jnp.concatenate([qkv_grad, extra_grads], axis=1), D).reshape(CD, 24, D)
    bias_grads = jnp.sum(projected_grad.astype(F32), axis=1).astype(BF)
    grads = jnp.concatenate(
        [
            main,
            out_grad.astype(BF).reshape(CD, 6, D),
            spread(bias_grads[:HW].reshape(CD, 1, 6), D),
            spread(bias_grads[2 * HW :].reshape(CD, 1, 6), D),
        ],
        axis=1,
    )
    totals = jnp.sum(swap_experts(grads).astype(F32), axis=0)
    dealt = swap_seq(totals[:24].reshape(NS, 6, D))
    extra = jnp.sum(dealt[:, :, 3 * HW : 3 * HW + CD + 3], axis=0)
    whole_qkv = dealt[:, :, : 3 * HW].reshape(NS, 6, 3, HW).transpose(1, 2, 0, 3).reshape(6, 3 * D)
    return (
        mixed.reshape(tokens.shape),
        input_grad.astype(BF).reshape(tokens.shape),
        whole_qkv,
        totals[24:30],
        extra[:, :CD],
        extra[:, CD],
        extra[:, CD + 1],
        totals[30, :6],
        totals[31, :6],
        extra[:, CD + 2],
        inner_grad.astype(F32)[None],
        outer_grad.astype(F32)[None],
    )


def solution(mesh):
    return jax.shard_map(
        per_device,
        mesh=mesh,
        in_specs=(
            P("dp", ("seq", "ctx"), None),
            P(("seq", "ctx", "dp"), None),
            P(("seq", "ctx", "dp"), None),
            P(("seq", "ctx", "dp"), None),
            P(("seq", "ctx", "dp")),
            P(("seq", "ctx", "dp")),
            P(("seq", "ctx", "dp")),
            P(("seq", "ctx", "dp")),
            P(("seq", "ctx", "dp")),
            P(("ctx", "dp"), None, "seq"),
            P(("ctx", "dp"), None, "seq"),
            P("dp", ("seq", "ctx"), None),
            P("dp", ("seq", "ctx"), None),
        ),
        out_specs=(
            P("dp", ("seq", "ctx"), None),
            P("dp", ("seq", "ctx"), None),
            P(("seq", "ctx", "dp"), None),
            P(("seq", "ctx", "dp"), None),
            P(("seq", "ctx", "dp"), None),
            P(("seq", "ctx", "dp")),
            P(("seq", "ctx", "dp")),
            P(("seq", "ctx", "dp")),
            P(("seq", "ctx", "dp")),
            P(("seq", "ctx", "dp")),
            P(("ctx", "dp"), None, "seq"),
            P(("ctx", "dp"), None, "seq"),
        ),
        check_vma=False,
    )
```

time: 1630 us -> 379 us (0.23); the launches traced: 1600 us -> 372 us
  blocking collectives: 566 us -> 59 us
  matrix products: 322 us -> 10.5 us
  local copies, waits for them, and re-layouts: 303 us -> 20.4 us
  starting transfers between devices: 195 us -> 54.4 us
  other arithmetic: 113 us -> 16.5 us
  Pallas kernels: 0 us -> 76.5 us
  waiting for transfers between devices: 83.3 us -> 120 us
    unnamed x3 -> x0, blocking collectives: 518 us -> none
    dot_general x159 -> x9, matrix products: 322 us -> 10.5 us  [dot(): lax.dot_general(former, latter, (((former_dim,), (latter_dim,)), ((), ())...]
    unnamed x65 -> x0, starting transfers between devices: 162 us -> none
    ppermute x0 -> x27, waiting for transfers between devices: none -> 91.6 us  [the longest x9 43.2 us: shift_seq(): lax.ppermute(values, 'seq', [(i, (i + steps) % NS) for i in range(NS)])]
    squeeze x80 -> x2, local copies, waits for them, and re-layouts: 83.7 us -> 0.56 us  [the longest x1 0.52 us: per_device(): totals[31, :6]]
    pallas_call x0 -> x7, Pallas kernels: none -> 76.5 us  [the longest x1 24.6 us: attend_back(): pl.pallas_call(attend_back_kernel, out_shape=[jax.ShapeDtypeStruct((HW, Q...]
    unnamed x138 -> x75, local copies, waits for them, and re-layouts: 76.4 us -> 6.83 us
    dynamic_slice x80 -> x0, local copies, waits for them, and re-layouts: 58.3 us -> none  [per_device(): lax.scan(track_peak, (start_peak, jnp.zeros((heads_here, block_rows), jnp...]
  transfers between devices with their start and end apart: 80 -> 35, of which waited for: 8 -> 25; matrix products, arithmetic and copies ran while one was open for 48% -> 11% of each run, Pallas kernels for 0% -> 15%
where the time goes in v1:
time: 379 us; the launch traced here: 372 us
  waiting for transfers between devices  120 us (32%)
  Pallas kernels  76.5 us (20%)
  blocking collectives  59 us (16%)
  starting transfers between devices  54.4 us (14%)
  local copies, waits for them, and re-layouts  20.4 us (5%)
  other arithmetic  16.5 us (4%)
  between operations  14.8 us (4%)
  matrix products  10.5 us (3%)
    all_to_all x2, blocking collectives, swap_experts(): lax.all_to_all(values, ('ctx', 'dp'), split_axis=0, concat_axis=0, tiled=...  49.3 us
    ppermute x9, waiting for transfers between devices, shift_seq(): lax.ppermute(values, 'seq', [(i, (i + steps) % NS) for i in range(NS)])  43.2 us
    ppermute x12, waiting for transfers between devices, shift_z(): return lax.ppermute(values, 'ctx', pairs)  31.3 us
    pallas_call x1, Pallas kernels, attend_back(): pl.pallas_call(attend_back_kernel, out_shape=[jax.ShapeDtypeStruct((HW, Q...  24.6 us
    pallas_call x1, Pallas kernels, expert(): pl.pallas_call(expert_kernel, grid=(NS * halves,), out_shape=[jax.ShapeDt...  21.8 us
    pallas_call x1, Pallas kernels, attend(): pl.pallas_call(attend_kernel, out_shape=[jax.ShapeDtypeStruct((PACK, QR),...  17.9 us
    ppermute x6, waiting for transfers between devices, shift_y(): return lax.ppermute(values, 'ctx', pairs)  17.1 us
    all_to_all x2, waiting for transfers between devices, swap_seq(): lax.all_to_all(values, 'seq', split_axis=0, concat_axis=0, tiled=True)  15.3 us
  transfers between devices with their start and end apart: 35, of which 25 were waited for; matrix products, arithmetic and copies ran while one was open for 11% of the time, Pallas kernels for 15%

profile of v1, /device:TPU:0, one launch (start us, length us, event | category | flops | bytes accessed | tf_op | source)
XLA Modules:
  0.0 372.5 jit_solution(7177267828454133703)
XLA Ops:
  9.5 9.7 %all_to_all.35 = bf16[4,6,768]{2,1,0:T(8,128)(2,1)S(1)} all-to-all(bf16[4,6,768]{2,1,0:T(8,128)(2,1)S(1)} %pad.22.clone), channel_id=1, replica_groups=mesh['seq'=4,'ctx'=16,'dp'=2] {'seq'}, dimensions={0} | all-to-all | bytes 73728 | tf_op jit(solution)/shard_map/all_to_all | solution.py:72
  20.6 8.5 %all-to-all-start.1 = ((bf16[32,32,768]{2,1,0:T(8,128)(2,1)}), bf16[32,32,768]{2,1,0:T(8,128)(2,1)S(1)}, u32[]{:S(2)}, u32[]{:S(2)}) async-start(bf16[32,32,768]{2,1,0:T(8,128)(2,1)} %broadcast_in_dim.67), calls=%async_computation.1 | async-start | bytes 3145728 | tf_op jit(solution)/shard_map/all_to_all | solution.py:76
  31.9 9.2 %collective-permute-done = bf16[128,768]{1,0:T(8,128)(2,1)S(1)} collective-permute-done((bf16[128,768]{1,0:T(8,128)(2,1)S(1)}, bf16[128,768]{1,0:T(8,128)(2,1)S(1)}, u32[]{:S(2)}, u32[]{:S(2)}) %collective-permute-start) | collective-permute-done | bytes 196640 | tf_op jit(solution)/shard_map/ppermute | solution.py:50
  43.8 5.6 %collective-permute-done.2 = bf16[128,768]{1,0:T(8,128)(2,1)S(1)} collective-permute-done((bf16[128,768]{1,0:T(8,128)(2,1)S(1)}, bf16[128,768]{1,0:T(8,128)(2,1)S(1)}, u32[]{:S(2)}, u32[]{:S(2)}) %collective-permute-start.2) | collective-permute-done | bytes 196640 | tf_op jit(solution)/shard_map/ppermute | solution.py:50
  67.3 6.3 %collective-permute-done.4.refs_2_ = bf16[192,512]{1,0:T(8,128)(2,1)} collective-permute-done((bf16[192,512]{1,0:T(8,128)(2,1)}, bf16[192,512]{1,0:T(8,128)(2,1)}, u32[]{:S(2)}, u32[]{:S(2)}) %collective-permute-start.4) | collective-permute-done | bytes 196640 | tf_op jit(solution)/shard_map/ppermute | solution.py:55
  75.6 3.8 %collective-permute-done.6.refs_5_ = bf16[384,512]{1,0:T(8,128)(2,1)} collective-permute-done((bf16[384,512]{1,0:T(8,128)(2,1)}, bf16[384,512]{1,0:T(8,128)(2,1)}, u32[]{:S(2)}, u32[]{:S(2)}) %collective-permute-start.6) | collective-permute-done | bytes 393248 | tf_op jit(solution)/shard_map/ppermute | solution.py:60
  79.5 3.7 collective-permute-done.8.refs_7_
  83.1 17.9 %attend.1 = (bf16[208,512]{1,0:T(8,128)(2,1)}, bf16[208,512]{1,0:T(8,128)(2,1)}, bf16[208,512]{1,0:T(8,128)(2,1)}, bf16[208,512]{1,0:T(8,128)(2,1)}) custom-call(s32[2]{0:T(128)} %pad_add_fusion.place_ref, bf16[192,512]{1,0:T(8,128)(2,1)} %slice_multiply_fusion.refs_0_, bf16[192,512]{1,0:T(8,128)(2,1)} %collective-permute-done.3.refs_1_, ...), custom_call_target="tpu_custom_call" | custom-call | flops 2013265920 | bytes 4194304 | tf_op jit(solution)/shard_map/attend/pallas_call | solution.py:161
  106.3 4.7 %collective-permute-done.10.refs_2_ = bf16[208,512]{1,0:T(8,128)(2,1)} collective-permute-done((bf16[208,512]{1,0:T(8,128)(2,1)}, bf16[208,512]{1,0:T(8,128)(2,1)}, u32[]{:S(2)}, u32[]{:S(2)}) %collective-permute-start.10) | collective-permute-done | bytes 213024 | tf_op jit(solution)/shard_map/ppermute | solution.py:55
  118.9 4.3 %all-to-all-start.2 = ((bf16[4,128,768]{2,1,0:T(8,128)(2,1)}), bf16[4,128,768]{2,1,0:T(8,128)(2,1)S(1)}, u32[]{:S(2)}, u32[]{:S(2)}) async-start(bf16[4,128,768]{2,1,0:T(8,128)(2,1)} %bitcast.16), calls=%async_computation.2 | async-start | bytes 1572864 | tf_op jit(solution)/shard_map/all_to_all | solution.py:72
  125.7 10.6 %all-to-all-done.2.branch_ref = bf16[4,128,768]{2,1,0:T(8,128)(2,1)S(1)} async-done(((bf16[4,128,768]{2,1,0:T(8,128)(2,1)}), bf16[4,128,768]{2,1,0:T(8,128)(2,1)S(1)}, u32[]{:S(2)}, u32[]{:S(2)}) %all-to-all-start.2) | async-done | bytes 786464 | tf_op jit(solution)/shard_map/all_to_all | solution.py:72
  137.2 3.9 %route.1 = (bf16[768,768]{1,0:T(8,128)(2,1)}, f32[128,768]{1,0:T(8,128)}, bf16[128,768]{1,0:T(8,128)(2,1)}, f32[128,2]{1,0:T(8,128)}, s32[128,2]{1,0:T(8,128)}) custom-call(bf16[128,768]{1,0:T(8,128)(2,1)} %bitcast.93, bf16[4,128,768]{2,1,0:T(8,128)(2,1)} %copy-done.5, f32[8,768]{1,0:T(8,128)} %copy-done.15, bf16[768,32]{1,0:T(8,128)(2,1)} %slice.119.router_ref, ...), custom_call_target="tpu_custom_call" | custom-call | tf_op jit(solution)/shard_map/route/pallas_call | solution.py:356
  141.0 26.4 %all_to_all.36 = bf16[32,24,768]{2,1,0:T(8,128)(2,1)} all-to-all(bf16[32,24,768]{2,1,0:T(8,128)(2,1)} %bitcast.106), channel_id=1, replica_groups=mesh['seq'=4,'ctx'=16,'dp'=2] {'ctx','dp'}, dimensions={0} | all-to-all | bytes 2359296 | tf_op jit(solution)/shard_map/all_to_all | solution.py:76
  167.4 21.8 %expert.1 = (bf16[768,768]{1,0:T(8,128)(2,1)}, bf16[4,768,768]{2,1,0:T(8,128)(2,1)}, bf16[4,768,768]{2,1,0:T(8,128)(2,1)}) custom-call(bf16[768,768]{1,0:T(8,128)(2,1)} %bitcast.105, bf16[576,768]{1,0:T(8,128)(2,1)} %constant.97.clone.pick_ref, bf16[4,768,768]{2,1,0:T(8,128)(2,1)} %all-gather.3.cloned.1.call-done.win_ref, ...), custom_call_target="tpu_custom_call" | custom-call | flops 8153726976 | bytes 20971520 | tf_op jit(solution)/shard_map/expert/pallas_call | solution.py:436
  190.6 22.9 %all_to_all.37 = bf16[32,24,768]{2,1,0:T(8,128)(2,1)} all-to-all(bf16[32,24,768]{2,1,0:T(8,128)(2,1)S(1)} %bitcast.104), channel_id=1, replica_groups=mesh['seq'=4,'ctx'=16,'dp'=2] {'ctx','dp'}, dimensions={0} | all-to-all | bytes 2359296 | tf_op jit(solution)/shard_map/all_to_all | solution.py:76
  213.6 3.9 %settle.1 = (bf16[128,768]{1,0:T(8,128)(2,1)}, bf16[128,768]{1,0:T(8,128)(2,1)}, f32[128,768]{1,0:T(8,128)}, f32[768,32]{1,0:T(8,128)}, f32[8,768]{1,0:T(8,128)}) custom-call(bf16[768,768]{1,0:T(8,128)(2,1)} %bitcast.98, f32[128,768]{1,0:T(8,128)} %get-tuple-element.46.m_ref, bf16[128,768]{1,0:T(8,128)(2,1)} %get-tuple-element.47.a_ref, ...), custom_call_target="tpu_custom_call" | custom-call | tf_op jit(solution)/shard_map/settle/pallas_call | solution.py:501
  221.8 7.8 %collective-permute-done.12 = bf16[128,768]{1,0:T(8,128)(2,1)S(1)} collective-permute-done((bf16[128,768]{1,0:T(8,128)(2,1)}, bf16[128,768]{1,0:T(8,128)(2,1)S(1)}, u32[]{:S(2)}, u32[]{:S(2)}) %collective-permute-start.12) | collective-permute-done | bytes 196640 | tf_op jit(solution)/shard_map/ppermute | solution.py:50
  229.6 3.3 collective-permute-done.13
  233.0 5.8 %collective-permute-done.14 = bf16[128,768]{1,0:T(8,128)(2,1)S(1)} collective-permute-done((bf16[128,768]{1,0:T(8,128)(2,1)}, bf16[128,768]{1,0:T(8,128)(2,1)S(1)}, u32[]{:S(2)}, u32[]{:S(2)}) %collective-permute-start.14) | collective-permute-done | bytes 196640 | tf_op jit(solution)/shard_map/ppermute | solution.py:50
  245.4 5.0 %collective-permute-done.15.refs_9_ = bf16[208,512]{1,0:T(8,128)(2,1)S(1)} collective-permute-done((bf16[208,512]{1,0:T(8,128)(2,1)}, bf16[208,512]{1,0:T(8,128)(2,1)S(1)}, u32[]{:S(2)}, u32[]{:S(2)}) %collective-permute-start.15) | collective-permute-done | bytes 213024 | tf_op jit(solution)/shard_map/ppermute | solution.py:55
  256.1 24.6 %attend_back.1 = (bf16[192,512]{1,0:T(8,128)(2,1)}, bf16[192,512]{1,0:T(8,128)(2,1)}, bf16[192,512]{1,0:T(8,128)(2,1)}, bf16[192,512]{1,0:T(8,128)(2,1)}, bf16[3...) custom-call(s32[2]{0:T(128)} %pad_add_fusion.place_ref, ...), custom_call_target="tpu_custom_call" | custom-call | flops 5033164800 | bytes 6291456 | tf_op jit(solution)/shard_map/attend_back/pallas_call | solution.py:289
  288.2 4.8 %collective-permute-done.18 = bf16[192,512]{1,0:T(8,128)(2,1)S(1)} collective-permute-done((bf16[192,512]{1,0:T(8,128)(2,1)}, bf16[192,512]{1,0:T(8,128)(2,1)S(1)}, u32[]{:S(2)}, u32[]{:S(2)}) %collective-permute-start.18) | collective-permute-done | bytes 196640 | tf_op jit(solution)/shard_map/ppermute | solution.py:55
  296.6 8.9 %collective-permute-done.21 = bf16[384,512]{1,0:T(8,128)(2,1)S(1)} collective-permute-done((bf16[384,512]{1,0:T(8,128)(2,1)}, bf16[384,512]{1,0:T(8,128)(2,1)S(1)}, u32[]{:S(2)}, u32[]{:S(2)}) %collective-permute-start.21) | collective-permute-done | bytes 393248 | tf_op jit(solution)/shard_map/ppermute | solution.py:60
  308.8 3.5 convolution_convert_fusion.1
  317.0 6.1 %all-to-all-start.5 = ((bf16[32,32,768]{2,1,0:T(8,128)(2,1)}), bf16[32,32,768]{2,1,0:T(8,128)(2,1)S(1)}, u32[]{:S(2)}, u32[]{:S(2)}) async-start(bf16[32,32,768]{2,1,0:T(8,128)(2,1)} %fusion.4), calls=%async_computation.5 | async-start | bytes 3145728 | tf_op jit(solution)/shard_map/all_to_all | solution.py:76
  328.3 3.5 collective-permute-done.24
  331.8 5.4 %collective-permute-done.25 = bf16[128,768]{1,0:T(8,128)(2,1)S(1)} collective-permute-done((bf16[128,768]{1,0:T(8,128)(2,1)S(1)}, bf16[128,768]{1,0:T(8,128)(2,1)S(1)}, u32[]{:S(2)}, u32[]{:S(2)}) %collective-permute-start.25) | collective-permute-done | bytes 196640 | tf_op jit(solution)/shard_map/ppermute | solution.py:50
  338.4 8.7 %all-to-all-done.5 = bf16[32,32,768]{2,1,0:T(8,128)(2,1)S(1)} async-done(((bf16[32,32,768]{2,1,0:T(8,128)(2,1)}), bf16[32,32,768]{2,1,0:T(8,128)(2,1)S(1)}, u32[]{:S(2)}, u32[]{:S(2)}) %all-to-all-start.5) | async-done | bytes 1572896 | tf_op jit(solution)/shard_map/all_to_all | solution.py:76
  347.9 4.3 %all-to-all-start.6 = ((f32[4,6,768]{2,1,0:T(8,128)}), f32[4,6,768]{2,1,0:T(8,128)S(1)}, u32[]{:S(2)}, u32[]{:S(2)}) async-start(f32[4,6,768]{2,1,0:T(8,128)} %reshape.190), calls=%async_computation.6 | async-start | bytes 196608 | tf_op jit(solution)/shard_map/all_to_all | solution.py:72
  353.4 4.7 %all-to-all-done.6 = f32[4,6,768]{2,1,0:T(8,128)S(1)} async-done(((f32[4,6,768]{2,1,0:T(8,128)}), f32[4,6,768]{2,1,0:T(8,128)S(1)}, u32[]{:S(2)}, u32[]{:S(2)}) %all-to-all-start.6) | async-done | bytes 73760 | tf_op jit(solution)/shard_map/all_to_all | solution.py:72
  359.8 2.8 convert_element_type.147
  362.7 2.8 convert_element_type.148
  (207 shorter events, 92.7 us)
Async XLA Ops:
  7.3 160.2 %all-gather.3.cloned.1.call-start = ((), (), s32[]{:S(2)}) async-start(), calls=%async_computation.9 | async-start | bytes 5898240 | tf_op jit(solution)/shard_map/all_gather | solution.py:552
  8.0 159.5 %all-gather.5.cloned.1.call-start = ((), (), s32[]{:S(2)}) async-start(), calls=%async_computation.10 | async-start | bytes 5898240 | tf_op jit(solution)/shard_map/all_gather | solution.py:553
  20.6 32.4 %all-to-all-start.1 = ((bf16[32,32,768]{2,1,0:T(8,128)(2,1)}), bf16[32,32,768]{2,1,0:T(8,128)(2,1)S(1)}, u32[]{:S(2)}, u32[]{:S(2)}) async-start(bf16[32,32,768]{2,1,0:T(8,128)(2,1)} %broadcast_in_dim.67), calls=%async_computation.1 | async-start | bytes 3145728 | tf_op jit(solution)/shard_map/all_to_all | solution.py:76
  29.1 12.0 %collective-permute-start = (bf16[128,768]{1,0:T(8,128)(2,1)S(1)}, bf16[128,768]{1,0:T(8,128)(2,1)S(1)}, u32[]{:S(2)}, u32[]{:S(2)}) collective-permute-start(bf16[128,768]{1,0:T(8,128)(2,1)S(1)} %bitcast.94), channel_id=1, source_target_pairs={{0,96},{32,0},{64,32},{96,64},{1,97},{33,1},{65,33},{97,65},{2,98}... | collective-permute-start | bytes 589832 | tf_op jit(solution)/shard_map/ppermute | solution.py:50
  30.4 13.4 %collective-permute-start.1 = (bf16[128,768]{1,0:T(8,128)(2,1)S(1)}, bf16[128,768]{1,0:T(8,128)(2,1)S(1)}, u32[]{:S(2)}, u32[]{:S(2)}) collective-permute-start(bf16[128,768]{1,0:T(8,128)(2,1)S(1)} %bitcast.95), channel_id=1, source_target_pairs={{0,64},{32,96},{64,0},{96,32},{1,65},{33,97},{65,1},{97,33},{2,66}... | collective-permute-start | bytes 589832 | tf_op jit(solution)/shard_map/ppermute | solution.py:50
  31.8 17.6 %collective-permute-start.2 = (bf16[128,768]{1,0:T(8,128)(2,1)S(1)}, bf16[128,768]{1,0:T(8,128)(2,1)S(1)}, u32[]{:S(2)}, u32[]{:S(2)}) collective-permute-start(bf16[128,768]{1,0:T(8,128)(2,1)S(1)} %bitcast.96), channel_id=1, source_target_pairs={{0,32},{32,64},{64,96},{96,0},{1,33},{33,65},{65,97},{97,1},{2,34}... | collective-permute-start | bytes 589832 | tf_op jit(solution)/shard_map/ppermute | solution.py:50
  61.0 18.5 %collective-permute-start.6 = (bf16[384,512]{1,0:T(8,128)(2,1)}, bf16[384,512]{1,0:T(8,128)(2,1)}, u32[]{:S(2)}, u32[]{:S(2)}) collective-permute-start(bf16[384,512]{1,0:T(8,128)(2,1)} %slice.117.refs_4_), channel_id=1, source_target_pairs={{0,6},{2,0},{4,2},{6,4},{8,14},{10,8},{12,10},{14,12},{16,22},{18,... | collective-permute-start | bytes 1179656 | tf_op jit(solution)/shard_map/ppermute | solution.py:60
  63.2 16.3 %collective-permute-start.7 = (bf16[384,512]{1,0:T(8,128)(2,1)}, bf16[384,512]{1,0:T(8,128)(2,1)}, u32[]{:S(2)}, u32[]{:S(2)}) collective-permute-start(bf16[384,512]{1,0:T(8,128)(2,1)} %slice.117.refs_4_), channel_id=1, source_target_pairs={{0,4},{2,6},{4,0},{6,2},{8,12},{10,14},{12,8},{14,10},{16,20},{18,... | collective-permute-start | bytes 1179656 | tf_op jit(solution)/shard_map/ppermute | solution.py:60
  64.0 19.1 %collective-permute-start.8 = (bf16[384,512]{1,0:T(8,128)(2,1)}, bf16[384,512]{1,0:T(8,128)(2,1)}, u32[]{:S(2)}, u32[]{:S(2)}) collective-permute-start(bf16[384,512]{1,0:T(8,128)(2,1)} %slice.117.refs_4_), channel_id=1, source_target_pairs={{0,2},{2,4},{4,6},{6,0},{8,10},{10,12},{12,14},{14,8},{16,18},{18,... | collective-permute-start | bytes 1179656 | tf_op jit(solution)/shard_map/ppermute | solution.py:60
  64.9 8.7 %collective-permute-start.4 = (bf16[192,512]{1,0:T(8,128)(2,1)}, bf16[192,512]{1,0:T(8,128)(2,1)}, u32[]{:S(2)}, u32[]{:S(2)}) collective-permute-start(bf16[192,512]{1,0:T(8,128)(2,1)} %slice_multiply_fusion.refs_0_), channel_id=1, source_target_pairs={{0,16},{2,18},{4,20},{6,22},{8,24},{10,26},{12,28},{14,30},{16,0},... | collective-permute-start | bytes 589832 | tf_op jit(solution)/shard_map/ppermute | solution.py:55
  65.7 9.9 %collective-permute-start.5 = (bf16[192,512]{1,0:T(8,128)(2,1)}, bf16[192,512]{1,0:T(8,128)(2,1)}, u32[]{:S(2)}, u32[]{:S(2)}) collective-permute-start(bf16[192,512]{1,0:T(8,128)(2,1)} %slice_multiply_fusion.refs_0_), channel_id=1, source_target_pairs={{0,8},{2,10},{4,12},{6,14},{8,16},{10,18},{12,20},{14,22},{16,24},... | collective-permute-start | bytes 589832 | tf_op jit(solution)/shard_map/ppermute | solution.py:55
  101.0 9.9 %collective-permute-start.10 = (bf16[208,512]{1,0:T(8,128)(2,1)}, bf16[208,512]{1,0:T(8,128)(2,1)}, u32[]{:S(2)}, u32[]{:S(2)}) collective-permute-start(bf16[208,512]{1,0:T(8,128)(2,1)} %get-tuple-element.41), channel_id=1, source_target_pairs={{0,16},{2,18},{4,20},{6,22},{8,24},{10,26},{12,28},{14,30},{16,0},... | collective-permute-start | bytes 638984 | tf_op jit(solution)/shard_map/ppermute | solution.py:55
  102.4 9.9 %collective-permute-start.11 = (bf16[208,512]{1,0:T(8,128)(2,1)}, bf16[208,512]{1,0:T(8,128)(2,1)}, u32[]{:S(2)}, u32[]{:S(2)}) collective-permute-start(bf16[208,512]{1,0:T(8,128)(2,1)} %get-tuple-element.42), channel_id=1, source_target_pairs={{0,24},{2,26},{4,28},{6,30},{8,0},{10,2},{12,4},{14,6},{16,8},{18,... | collective-permute-start | bytes 638984 | tf_op jit(solution)/shard_map/ppermute | solution.py:55
  104.4 10.2 %collective-permute-start.9 = (bf16[208,512]{1,0:T(8,128)(2,1)}, bf16[208,512]{1,0:T(8,128)(2,1)}, u32[]{:S(2)}, u32[]{:S(2)}) collective-permute-start(bf16[208,512]{1,0:T(8,128)(2,1)} %get-tuple-element.40), channel_id=1, source_target_pairs={{0,8},{2,10},{4,12},{6,14},{8,16},{10,18},{12,20},{14,22},{16,24},... | collective-permute-start | bytes 638984 | tf_op jit(solution)/shard_map/ppermute | solution.py:55
  118.9 17.4 %all-to-all-start.2 = ((bf16[4,128,768]{2,1,0:T(8,128)(2,1)}), bf16[4,128,768]{2,1,0:T(8,128)(2,1)S(1)}, u32[]{:S(2)}, u32[]{:S(2)}) async-start(bf16[4,128,768]{2,1,0:T(8,128)(2,1)} %bitcast.16), calls=%async_computation.2 | async-start | bytes 1572864 | tf_op jit(solution)/shard_map/all_to_all | solution.py:72
  123.2 236.6 %reduce-scatter.3.cloned.1.call-start = ((), (), s32[]{:S(2)}) async-start(), calls=%async_computation.11 | async-start | bytes 5898240 | tf_op jit(solution)/shard_map/reduce_scatter | solution.py:595
  189.3 173.3 %reduce-scatter.5.cloned.1.call-start = ((), (), s32[]{:S(2)}) async-start(), calls=%async_computation.12 | async-start | bytes 5898240 | tf_op jit(solution)/shard_map/reduce_scatter | solution.py:596
  217.4 12.2 %collective-permute-start.12 = (bf16[128,768]{1,0:T(8,128)(2,1)}, bf16[128,768]{1,0:T(8,128)(2,1)S(1)}, u32[]{:S(2)}, u32[]{:S(2)}) collective-permute-start(bf16[128,768]{1,0:T(8,128)(2,1)} %get-tuple-element.52), channel_id=1, source_target_pairs={{0,96},{32,0},{64,32},{96,64},{1,97},{33,1},{65,33},{97,65},{2,98}... | collective-permute-start | bytes 589832 | tf_op jit(solution)/shard_map/ppermute | solution.py:50
  219.3 13.7 %collective-permute-start.13 = (bf16[128,768]{1,0:T(8,128)(2,1)}, bf16[128,768]{1,0:T(8,128)(2,1)S(1)}, u32[]{:S(2)}, u32[]{:S(2)}) collective-permute-start(bf16[128,768]{1,0:T(8,128)(2,1)} %get-tuple-element.52), channel_id=1, source_target_pairs={{0,64},{32,96},{64,0},{96,32},{1,65},{33,97},{65,1},{97,33},{2,66}... | collective-permute-start | bytes 589832 | tf_op jit(solution)/shard_map/ppermute | solution.py:50
  220.8 17.9 %collective-permute-start.14 = (bf16[128,768]{1,0:T(8,128)(2,1)}, bf16[128,768]{1,0:T(8,128)(2,1)S(1)}, u32[]{:S(2)}, u32[]{:S(2)}) collective-permute-start(bf16[128,768]{1,0:T(8,128)(2,1)} %get-tuple-element.52), channel_id=1, source_target_pairs={{0,32},{32,64},{64,96},{96,0},{1,33},{33,65},{65,97},{97,1},{2,34}... | collective-permute-start | bytes 589832 | tf_op jit(solution)/shard_map/ppermute | solution.py:50
  243.1 9.9 %collective-permute-start.16 = (bf16[208,512]{1,0:T(8,128)(2,1)}, bf16[208,512]{1,0:T(8,128)(2,1)S(1)}, u32[]{:S(2)}, u32[]{:S(2)}) collective-permute-start(bf16[208,512]{1,0:T(8,128)(2,1)} %grad_heads.1.refs_8_), channel_id=1, source_target_pairs={{0,16},{2,18},{4,20},{6,22},{8,24},{10,26},{12,28},{14,30},{16,0},... | collective-permute-start | bytes 638984 | tf_op jit(solution)/shard_map/ppermute | solution.py:55
  244.7 10.7 %collective-permute-start.17 = (bf16[208,512]{1,0:T(8,128)(2,1)}, bf16[208,512]{1,0:T(8,128)(2,1)S(1)}, u32[]{:S(2)}, u32[]{:S(2)}) collective-permute-start(bf16[208,512]{1,0:T(8,128)(2,1)} %grad_heads.1.refs_8_), channel_id=1, source_target_pairs={{0,8},{2,10},{4,12},{6,14},{8,16},{10,18},{12,20},{14,22},{16,24},... | collective-permute-start | bytes 638984 | tf_op jit(solution)/shard_map/ppermute | solution.py:55
  280.7 12.3 %collective-permute-start.18 = (bf16[192,512]{1,0:T(8,128)(2,1)}, bf16[192,512]{1,0:T(8,128)(2,1)S(1)}, u32[]{:S(2)}, u32[]{:S(2)}) collective-permute-start(bf16[192,512]{1,0:T(8,128)(2,1)} %get-tuple-element.55), channel_id=1, source_target_pairs={{0,8},{2,10},{4,12},{6,14},{8,16},{10,18},{12,20},{14,22},{16,24},... | collective-permute-start | bytes 589832 | tf_op jit(solution)/shard_map/ppermute | solution.py:55
  281.7 13.4 %collective-permute-start.19 = (bf16[192,512]{1,0:T(8,128)(2,1)}, bf16[192,512]{1,0:T(8,128)(2,1)}, u32[]{:S(2)}, u32[]{:S(2)}) collective-permute-start(bf16[192,512]{1,0:T(8,128)(2,1)} %get-tuple-element.56), channel_id=1, source_target_pairs={{0,16},{2,18},{4,20},{6,22},{8,24},{10,26},{12,28},{14,30},{16,0},... | collective-permute-start | bytes 589832 | tf_op jit(solution)/shard_map/ppermute | solution.py:55
  283.8 11.3 %collective-permute-start.20 = (bf16[192,512]{1,0:T(8,128)(2,1)}, bf16[192,512]{1,0:T(8,128)(2,1)}, u32[]{:S(2)}, u32[]{:S(2)}) collective-permute-start(bf16[192,512]{1,0:T(8,128)(2,1)} %get-tuple-element.57), channel_id=1, source_target_pairs={{0,24},{2,26},{4,28},{6,30},{8,0},{10,2},{12,4},{14,6},{16,8},{18,... | collective-permute-start | bytes 589832 | tf_op jit(solution)/shard_map/ppermute | solution.py:55
  285.5 20.0 %collective-permute-start.21 = (bf16[384,512]{1,0:T(8,128)(2,1)}, bf16[384,512]{1,0:T(8,128)(2,1)S(1)}, u32[]{:S(2)}, u32[]{:S(2)}) collective-permute-start(bf16[384,512]{1,0:T(8,128)(2,1)} %get-tuple-element.59), channel_id=1, source_target_pairs={{0,2},{2,4},{4,6},{6,0},{8,10},{10,12},{12,14},{14,8},{16,18},{18,... | collective-permute-start | bytes 1179656 | tf_op jit(solution)/shard_map/ppermute | solution.py:60
  286.1 19.4 %collective-permute-start.22 = (bf16[384,512]{1,0:T(8,128)(2,1)}, bf16[384,512]{1,0:T(8,128)(2,1)}, u32[]{:S(2)}, u32[]{:S(2)}) collective-permute-start(bf16[384,512]{1,0:T(8,128)(2,1)} %get-tuple-element.60), channel_id=1, source_target_pairs={{0,4},{2,6},{4,0},{6,2},{8,12},{10,14},{12,8},{14,10},{16,20},{18,... | collective-permute-start | bytes 1179656 | tf_op jit(solution)/shard_map/ppermute | solution.py:60
  293.6 12.5 %collective-permute-start.23 = (bf16[384,512]{1,0:T(8,128)(2,1)}, bf16[384,512]{1,0:T(8,128)(2,1)}, u32[]{:S(2)}, u32[]{:S(2)}) collective-permute-start(bf16[384,512]{1,0:T(8,128)(2,1)} %get-tuple-element.61), channel_id=1, source_target_pairs={{0,6},{2,0},{4,2},{6,4},{8,14},{10,8},{12,10},{14,12},{16,22},{18,... | collective-permute-start | bytes 1179656 | tf_op jit(solution)/shard_map/ppermute | solution.py:60
  317.0 30.0 %all-to-all-start.5 = ((bf16[32,32,768]{2,1,0:T(8,128)(2,1)}), bf16[32,32,768]{2,1,0:T(8,128)(2,1)S(1)}, u32[]{:S(2)}, u32[]{:S(2)}) async-start(bf16[32,32,768]{2,1,0:T(8,128)(2,1)} %fusion.4), calls=%async_computation.5 | async-start | bytes 3145728 | tf_op jit(solution)/shard_map/all_to_all | solution.py:76
  325.5 11.6 %collective-permute-start.25 = (bf16[128,768]{1,0:T(8,128)(2,1)S(1)}, bf16[128,768]{1,0:T(8,128)(2,1)S(1)}, u32[]{:S(2)}, u32[]{:S(2)}) collective-permute-start(bf16[128,768]{1,0:T(8,128)(2,1)S(1)} %get-tuple-element.75), channel_id=1, source_target_pairs={{0,64},{32,96},{64,0},{96,32},{1,65},{33,97},{65,1},{97,33},{2,66}... | collective-permute-start | bytes 589832 | tf_op jit(solution)/shard_map/ppermute | solution.py:50
  327.9 9.3 %collective-permute-start.26 = (bf16[128,768]{1,0:T(8,128)(2,1)S(1)}, bf16[128,768]{1,0:T(8,128)(2,1)S(1)}, u32[]{:S(2)}, u32[]{:S(2)}) collective-permute-start(bf16[128,768]{1,0:T(8,128)(2,1)S(1)} %get-tuple-element.74), channel_id=1, source_target_pairs={{0,96},{32,0},{64,32},{96,64},{1,97},{33,1},{65,33},{97,65},{2,98}... | collective-permute-start | bytes 589832 | tf_op jit(solution)/shard_map/ppermute | solution.py:50
  347.9 10.2 %all-to-all-start.6 = ((f32[4,6,768]{2,1,0:T(8,128)}), f32[4,6,768]{2,1,0:T(8,128)S(1)}, u32[]{:S(2)}, u32[]{:S(2)}) async-start(f32[4,6,768]{2,1,0:T(8,128)} %reshape.190), calls=%async_computation.6 | async-start | bytes 196608 | tf_op jit(solution)/shard_map/all_to_all | solution.py:72
  (39 other events, 260.3 us)
Sparse Core Ops, SparseCore 0:
  9.8 63.4 all-gather.2
  74.9 53.5 all-gather.4
  189.4 56.0 reduce-scatter.2
  247.8 50.8 reduce-scatter.4
